TPU v7x, 32 devices: a whole 2x2x4 slice. The times are simulated.
32 devices in a mesh: rep: 4 (over y, x), wide: 8 (over z, core).
Axes of the slice: x: 2, y: 2, z: 4, core: 2. Of those that a mesh axis runs over, the one named last changes fastest.
Arguments:
- token_ids: int32 [4, 1, 2, 1, 2048], P('rep'), may hold values from 0 to 50303, as said below
- prompt_mask: int32 [4, 1, 2, 1, 2048], P('rep'), may hold values from 0 to 1, as said below
- loss_pos: int32 [4, 1, 2, 8, 16], P('rep'), may hold values from 0 to 254
- tables: float32 [2, 50304, 512], P(None, 'wide', 'rep'), may hold values from -12 to 12
- attention: float32 [2, 2, 512, 512], P(None, None, 'wide', 'rep')
- feedforward: float32 [2, 2, 512, 2048], P(None, None, 'wide', 'rep')
- key_value: float32 [512, 128], P('wide', 'rep'), may hold values from -0.25 to 0.25
- gains_biases: float32 [12416], P('rep')
- first_tables: float32 [4, 2, 50304, 512], P('rep', None, 'wide'), may hold values from -5.8365434e-06 to 5.8365434e-06
- first_attention: float32 [4, 2, 2, 512, 512], P('rep', None, None, 'wide'), may hold values from -2.2888184e-05 to 2.2888184e-05
- first_feedforward: float32 [4, 2, 2, 512, 2048], P('rep', None, None, 'wide'), may hold values from -2.2888184e-05 to 2.2888184e-05
- first_key_value: float32 [4, 512, 128], P('rep', 'wide'), may hold values from -2.2888184e-05 to 2.2888184e-05
- first_gains: float32 [4, 12416], P('rep'), may hold values from -9.1552734e-05 to 9.1552734e-05
- second_tables: float32 [4, 2, 50304, 512], P('rep', None, 'wide'), may hold values from 9.2553283e-14 to 3.69509303e-11
- second_attention: float32 [4, 2, 2, 512, 512], P('rep', None, None, 'wide'), may hold values from 9.255328e-12 to 3.6950932e-11
- second_feedforward: float32 [4, 2, 2, 512, 2048], P('rep', None, None, 'wide'), may hold values from 9.255328e-12 to 3.6950932e-11
- second_key_value: float32 [4, 512, 128], P('rep', 'wide'), may hold values from 9.255328e-12 to 3.6950932e-11
- second_gains: float32 [4, 12416], P('rep'), may hold values from 1.759568e-10 to 7.038272e-10
- outer_tables: float32 [2, 50304, 512], P(None, 'wide', 'rep'), may hold values from -0.3125 to 0.3125
- outer_attention: float32 [2, 2, 512, 512], P(None, None, 'wide', 'rep'), may hold values from -0.3125 to 0.3125
- outer_feedforward: float32 [2, 2, 512, 2048], P(None, None, 'wide', 'rep'), may hold values from -0.3125 to 0.3125
- outer_key_value: float32 [512, 128], P('wide', 'rep'), may hold values from -0.3125 to 0.3125
- outer_gains: float32 [12416], P('rep'), may hold values from -0.3125 to 0.3125
Outputs:
- loss_sum: float32 [4], P('rep')
- loss_count: float32 [4], P('rep')
- new_tables: float32 [2, 50304, 512], P(None, 'wide', 'rep')
- new_attention: float32 [2, 2, 512, 512], P(None, None, 'wide', 'rep')
- new_feedforward: float32 [2, 2, 512, 2048], P(None, None, 'wide', 'rep')
- new_key_value: float32 [512, 128], P('wide', 'rep')
- new_gains: float32 [12416], P('rep')
- next_first_tables: float32 [4, 2, 50304, 512], P('rep', None, 'wide')
- next_first_attention: float32 [4, 2, 2, 512, 512], P('rep', None, None, 'wide')
- next_first_feedforward: float32 [4, 2, 2, 512, 2048], P('rep', None, None, 'wide')
- next_first_key_value: float32 [4, 512, 128], P('rep', 'wide')
- next_first_gains: float32 [4, 12416], P('rep')
- next_second_tables: float32 [4, 2, 50304, 512], P('rep', None, 'wide')
- next_second_attention: float32 [4, 2, 2, 512, 512], P('rep', None, None, 'wide')
- next_second_feedforward: float32 [4, 2, 2, 512, 2048], P('rep', None, None, 'wide')
- next_second_key_value: float32 [4, 512, 128], P('rep', 'wide')
- next_second_gains: float32 [4, 12416], P('rep')
- next_outer_tables: float32 [2, 50304, 512], P(None, 'wide', 'rep')
- next_outer_attention: float32 [2, 2, 512, 512], P(None, None, 'wide', 'rep')
- next_outer_feedforward: float32 [2, 2, 512, 2048], P(None, None, 'wide', 'rep')
- next_outer_key_value: float32 [512, 128], P('wide', 'rep')
- next_outer_gains: float32 [12416], P('rep')
Inputs may be any that keep to these rules, and one draw needn't show every extreme that they name: In each sequence prompt_mask is 0 before a prompt length under 2 * 2048 / 3 and 1 from there on. `token_ids`: vocabulary shard q holds the ids q * 6288 to (q + 1) * 6288 - 1. The 256 tokens of one device of wide in a micro-batch (places w * 256 to (w + 1) * 256 - 1 of every sequence) hold at most 64 ids of one shard, and in every micro-batch of a group some shard holds exactly 64 ids of every device's tokens.
All inputs are finite; a program needn't handle non-finite values.
Results may differ from a plain program's by a relative error of at most 0.012.
The roundings to bfloat16 on the way count: a program that leaves them out, or rounds other values in their place, can miss the bound.
Values may be sent and summed in bfloat16 or wider, within the bound.
No kernel may reach another device: no remote copies, remote signals or barrier semaphores. Data moves between devices by JAX's collectives and lax.ppermute only.
A program may use at most 448 MiB of HBM per device.

v0:
```python
from functools import partial

import jax
import jax.numpy as jnp
from jax import lax
from jax.sharding import PartitionSpec as P

D = 512
HEADS = 8
HD = 64
ROT = 16
FF = 2048
L = 2
GROUPS = 4
LEN = 2048
MICRO = 2
STEP = 5


NORM_EPSILON = 1e-05
CLIP = 0.1
LEARN_RATES = (0.02, 0.2, 0.02, 0.02, 0.2)
BETA_ONE = 0.9
BETA_TWO = 0.95
ADAM_EPSILON = 1e-08
DECAY = 0.1
OUTER_RATE = 0.7
OUTER_MOMENTUM = 0.9


def combined_all(value, axis, combine):
    everything = jax.tree.map(lambda part: lax.all_gather(part, axis), value)
    leading = jax.tree.map(lambda part: part[0], everything)

    def lap(k, so_far):
        return combine(so_far, jax.tree.map(lambda part: part[k], everything))

    return lax.fori_loop(1, lax.axis_size(axis), lap, leading)


def norm_forward(stream, gain, bias):
    centred = stream - jnp.mean(stream, axis=-1, keepdims=True)
    scale = lax.rsqrt(jnp.mean(centred * centred, axis=-1, keepdims=True) + NORM_EPSILON)
    normal = centred * scale
    return (normal * gain + bias, normal, scale)


def norm_backward(grad_out, normal, scale, gain):
    shaped = grad_out * gain
    grad_in = scale * (
        shaped
        - jnp.mean(shaped, axis=-1, keepdims=True)
        - normal * jnp.mean(shaped * normal, axis=-1, keepdims=True)
    )
    return (grad_in, jnp.sum(grad_out * normal, axis=0), jnp.sum(grad_out, axis=0))


def rotary_tables(places):
    frequency = 10000.0 ** (-2.0 * jnp.arange(ROT // 2, dtype=jnp.float32) / ROT)
    angles = places[:, None] * frequency[None, :]
    return (jnp.cos(angles), jnp.sin(angles))


def rotate(values, cosine_table, sine_table):
    half_dim = ROT // 2
    leading = values[..., :half_dim]
    trailing = values[..., half_dim:ROT]
    cosine = cosine_table[:, None, :]
    sine_part = sine_table[:, None, :]
    return jnp.concatenate(
        [
            leading * cosine - trailing * sine_part,
            trailing * cosine + leading * sine_part,
            values[..., ROT:],
        ],
        axis=-1,
    )


def unpack_small(gains_biases):
    span = 7 * D + FF
    layers = gains_biases[: L * span].reshape(L, span)
    remain = gains_biases[L * span :]
    return (layers, remain[: 2 * HD], remain[2 * HD : 2 * HD + D], remain[2 * HD + D :])


def to_heads(values):
    seq_count, rows_seq, _ = values.shape
    width = lax.axis_size("wide")
    bands = width // GROUPS
    pieces = values.reshape(seq_count, bands, rows_seq // bands, GROUPS, D // GROUPS).transpose(
        3, 1, 0, 2, 4
    )
    pieces = pieces.reshape(width, seq_count, rows_seq // bands, D // GROUPS)
    return lax.all_to_all(pieces, "wide", split_axis=0, concat_axis=0, tiled=True)


def to_tokens(values):
    back = lax.all_to_all(values, "wide", split_axis=0, concat_axis=0, tiled=True)
    width, seq_count, band_rows, group_width = back.shape
    back = back.reshape(GROUPS, width // GROUPS, seq_count, band_rows, group_width).transpose(
        2, 1, 3, 0, 4
    )
    return back.reshape(seq_count * (width // GROUPS) * band_rows, GROUPS * group_width)


def masked_scores(queries, pairs, query_places):
    scores = (
        jnp.einsum("qhd,kd->hqk", queries, pairs[:, :HD], preferred_element_type=jnp.float32)
        * 0.125
    )
    allowed = query_places[:, None] >= jnp.arange(pairs.shape[0])[None, :]
    return jnp.where(allowed[None], scores, -1e30)


def attend_forward(query_places, inputs):
    queries, pairs = inputs
    scores = masked_scores(queries, pairs, query_places)
    top = jnp.max(scores, axis=2, keepdims=True)
    expo = jnp.exp(scores - top)
    total = jnp.sum(expo, axis=2, keepdims=True)
    probs = (expo / total).astype(jnp.bfloat16)
    context = jnp.einsum("hqk,kd->qhd", probs, pairs[:, HD:], preferred_element_type=jnp.float32)
    return (
        context.astype(jnp.bfloat16).reshape(queries.shape[0], -1),
        (top + jnp.log(total))[..., 0],
    )


def attend_backward(query_places, inputs):
    queries, pairs, log_totals, grad_context = inputs
    scores = masked_scores(queries, pairs, query_places)
    probs = jnp.exp(scores - log_totals[..., None])
    grad_probs = jnp.einsum(
        "qhd,kd->hqk", grad_context, pairs[:, HD:], preferred_element_type=jnp.float32
    )
    inner = jnp.sum(probs * grad_probs, axis=2, keepdims=True)
    grad_scores = (probs * (grad_probs - inner)).astype(jnp.bfloat16)
    grad_queries = (
        jnp.einsum("hqk,kd->qhd", grad_scores, pairs[:, :HD], preferred_element_type=jnp.float32)
        * 0.125
    )
    grad_keys = (
        jnp.einsum("hqk,qhd->kd", grad_scores, queries, preferred_element_type=jnp.float32) * 0.125
    )
    grad_values = jnp.einsum(
        "hqk,qhd->kd", probs.astype(jnp.bfloat16), grad_context, preferred_element_type=jnp.float32
    )
    grad_queries = grad_queries.astype(jnp.bfloat16).reshape(queries.shape[0], -1)
    return (grad_queries, jnp.concatenate([grad_keys, grad_values], axis=1))


def per_sequence(received):
    width, seq_count, band_rows, group_width = received.shape
    return received.transpose(1, 0, 2, 3).reshape(
        seq_count, width * band_rows, group_width // HD, HD
    )


def from_sequence(values, like):
    width, seq_count, band_rows, group_width = like.shape
    return values.reshape(seq_count, width, band_rows, group_width).transpose(1, 0, 2, 3)


def layer_forward(stream, vectors, weights_layer, shared, pair_low, pair_bias, setting):
    cosine_table, sine_table, query_places, seq_count, rows_seq, vocab_rows, device = setting
    query_weight, out_weight, up_weight, down_weight = weights_layer
    normed, normal_attend, scale_attend = norm_forward(stream, vectors[0:D], vectors[D : 2 * D])
    feed_input, normal_feed, scale_feed = norm_forward(
        stream, vectors[2 * D : 3 * D], vectors[3 * D : 4 * D]
    )
    normed = normed.astype(jnp.bfloat16)
    feed_input = feed_input.astype(jnp.bfloat16)
    queries = (
        jnp.dot(normed, query_weight, preferred_element_type=jnp.float32) + vectors[4 * D : 5 * D]
    )
    queries = rotate(queries.reshape(-1, HEADS, HD), cosine_table, sine_table).astype(jnp.bfloat16)
    if shared is None:
        projected = jnp.dot(normed, pair_low, preferred_element_type=jnp.float32) + pair_bias
        turned = rotate(projected[:, None, :HD], cosine_table, sine_table)[:, 0]
        pairs = jnp.concatenate([turned, projected[:, HD:]], axis=1).astype(jnp.bfloat16)
        shared = lax.all_gather(
            pairs.reshape(seq_count, rows_seq, 2 * HD), "wide", axis=1, tiled=True
        )
    received = to_heads(queries.reshape(seq_count, rows_seq, D))
    context_seq, log_totals = lax.map(
        partial(attend_forward, query_places), (per_sequence(received), shared)
    )
    context = to_tokens(from_sequence(context_seq, received))
    branch = (
        jnp.dot(context, out_weight, preferred_element_type=jnp.float32) + vectors[5 * D : 6 * D]
    )
    hidden = jnp.dot(feed_input, up_weight, preferred_element_type=jnp.float32) + vectors[7 * D :]
    active = jax.nn.gelu(hidden, approximate=False).astype(jnp.bfloat16)
    output = (
        jnp.einsum("tf,df->td", active, down_weight, preferred_element_type=jnp.float32)
        + vectors[6 * D : 7 * D]
    )
    kept = (
        normed,
        feed_input,
        normal_attend,
        scale_attend,
        normal_feed,
        scale_feed,
        received,
        log_totals,
        context,
        hidden,
        active,
    )
    return (stream + branch + output, kept, shared)


def layer_backward(
    grad_stream, grad_shared, vectors, weights_layer, kept, shared, pair_low, setting, producer
):
    cosine_table, sine_table, query_places, seq_count, rows_seq, vocab_rows, device = setting
    query_weight, out_weight, up_weight, down_weight = weights_layer
    (
        normed,
        feed_input,
        normal_attend,
        scale_attend,
        normal_feed,
        scale_feed,
        received,
        log_totals,
        context,
        hidden,
        active,
    ) = kept
    grad_low = grad_stream.astype(jnp.bfloat16)
    grad_bias_out = jnp.sum(grad_low, axis=0, dtype=jnp.float32)
    grad_down = jnp.einsum("td,tf->df", grad_low, active, preferred_element_type=jnp.float32)
    grad_active = jnp.dot(grad_low, down_weight, preferred_element_type=jnp.float32)
    unused, gelu_pull = jax.vjp(partial(jax.nn.gelu, approximate=False), hidden)
    grad_hidden = gelu_pull(grad_active)[0].astype(jnp.bfloat16)
    grad_bias_up = jnp.sum(grad_hidden, axis=0, dtype=jnp.float32)
    grad_up = jnp.einsum("td,tf->df", feed_input, grad_hidden, preferred_element_type=jnp.float32)
    grad_feed = jnp.einsum("tf,df->td", grad_hidden, up_weight, preferred_element_type=jnp.float32)
    grad_out = jnp.einsum("td,te->de", context, grad_low, preferred_element_type=jnp.float32)
    grad_context = jnp.einsum(
        "te,de->td", grad_low, out_weight, preferred_element_type=jnp.float32
    ).astype(jnp.bfloat16)
    grad_received = to_heads(grad_context.reshape(seq_count, rows_seq, D))
    grad_seq, grad_pairs = lax.map(
        partial(attend_backward, query_places),
        (per_sequence(received), shared, log_totals, per_sequence(grad_received)),
    )
    grad_shared = grad_shared + grad_pairs
    grad_queries = (
        to_tokens(from_sequence(grad_seq, received)).astype(jnp.float32).reshape(-1, HEADS, HD)
    )
    grad_queries = (
        rotate(grad_queries, cosine_table, -sine_table).reshape(-1, D).astype(jnp.bfloat16)
    )
    grad_bias_query = jnp.sum(grad_queries, axis=0, dtype=jnp.float32)
    grad_query = jnp.einsum("td,te->de", normed, grad_queries, preferred_element_type=jnp.float32)
    grad_normed = jnp.einsum(
        "te,de->td", grad_queries, query_weight, preferred_element_type=jnp.float32
    )
    grad_pair = None
    grad_pair_bias = None
    if producer:
        total_pairs = lax.psum_scatter(grad_shared, "wide", scatter_dimension=1, tiled=True)
        total_pairs = total_pairs.reshape(-1, 2 * HD).astype(jnp.bfloat16).astype(jnp.float32)
        turned = rotate(total_pairs[:, None, :HD], cosine_table, -sine_table)[:, 0]
        grad_projected = jnp.concatenate([turned, total_pairs[:, HD:]], axis=1).astype(jnp.bfloat16)
        grad_pair_bias = jnp.sum(grad_projected, axis=0, dtype=jnp.float32)
        grad_pair = jnp.einsum(
            "td,te->de", normed, grad_projected, preferred_element_type=jnp.float32
        )
        grad_normed = grad_normed + jnp.einsum(
            "te,de->td", grad_projected, pair_low, preferred_element_type=jnp.float32
        )
    grad_attend, gain_attend, bias_attend = norm_backward(
        grad_normed, normal_attend, scale_attend, vectors[0:D]
    )
    grad_feed_in, gain_feed, bias_feed = norm_backward(
        grad_feed, normal_feed, scale_feed, vectors[2 * D : 3 * D]
    )
    grad_vector = jnp.concatenate(
        [
            gain_attend,
            bias_attend,
            gain_feed,
            bias_feed,
            grad_bias_query,
            grad_bias_out,
            grad_bias_out,
            grad_bias_up,
        ]
    )
    grads_layer = (grad_query, grad_out, grad_up, grad_down, grad_pair, grad_pair_bias, grad_vector)
    return (grad_stream + grad_attend + grad_feed_in, grad_shared, grads_layer)


def loss_rows(loss_now, width, rows_seq):
    seq_index = loss_now // (rows_seq - 1)
    place_index = jnp.arange(width, dtype=jnp.int32)[:, None] * rows_seq + loss_now % (rows_seq - 1)
    return (seq_index.reshape(-1), place_index.reshape(-1))


def embed_term(ordered, table_low, offset):
    chosen = ordered - offset
    inside = (chosen >= 0) & (chosen < table_low.shape[0])
    picked = table_low[jnp.clip(chosen, 0, table_low.shape[0] - 1)]
    return jnp.where(inside[:, None], picked.astype(jnp.float32), 0.0)


def embed_add(ordered, offset, carry, piece):
    chosen = ordered - offset
    inside = (chosen >= 0) & (chosen < carry.shape[0])
    return carry.at[jnp.clip(chosen, 0, carry.shape[0] - 1)].add(
        jnp.where(inside[:, None], piece, 0.0)
    )


def head_term(grad_logits, unembed_low):
    return jnp.dot(grad_logits, unembed_low, preferred_element_type=jnp.float32)


def combine_parts(former, latter):
    top = jnp.maximum(former[0], latter[0])
    total = former[1] * jnp.exp(former[0] - top) + latter[1] * jnp.exp(latter[0] - top)
    return (top, total, former[2] + latter[2])


def micro_pass(token_now, mask_now, loss_now, weights_now, setting, denominator):
    (
        table_low,
        attention_low,
        feed_low,
        pair_low,
        layer_vectors,
        pair_bias,
        final_gain,
        final_bias,
    ) = weights_now
    cosine_table, sine_table, query_places, seq_count, rows_seq, vocab_rows, device = setting
    width = lax.axis_size("wide")
    offset = device * vocab_rows
    ordered = token_now.reshape(seq_count, width, rows_seq).transpose(1, 0, 2).reshape(-1)
    stream = lax.psum_scatter(
        embed_term(ordered, table_low[0], offset).astype(jnp.bfloat16),
        "wide",
        scatter_dimension=0,
        tiled=True,
    ).astype(jnp.float32)
    shared = None
    kept_all = []
    layer_weights = []
    for layer_number in range(L):
        weights_layer = (
            attention_low[layer_number, 0],
            attention_low[layer_number, 1],
            feed_low[layer_number, 0],
            feed_low[layer_number, 1],
        )
        layer_weights.append(weights_layer)
        stream, kept, shared = layer_forward(
            stream, layer_vectors[layer_number], weights_layer, shared, pair_low, pair_bias, setting
        )
        kept_all.append(kept)
    final_norm, final_normal, final_scale = norm_forward(stream, final_gain, final_bias)
    seq_index, place_index = loss_rows(loss_now, width, rows_seq)
    own_codes = loss_now[device]
    mine = own_codes // (rows_seq - 1) * rows_seq + own_codes % (rows_seq - 1)
    gathered = lax.all_gather(final_norm[mine].astype(jnp.bfloat16), "wide", axis=0, tiled=True)
    targets = token_now[seq_index, place_index + 1]
    weight = mask_now[seq_index, place_index + 1].astype(jnp.float32)
    logits = jnp.einsum("rd,vd->rv", gathered, table_low[1], preferred_element_type=jnp.float32)
    local_target = targets - offset
    hits = jnp.arange(vocab_rows, dtype=jnp.int32)[None, :] == local_target[:, None]
    target_logit = jnp.sum(jnp.where(hits, logits, 0.0), axis=1)
    top = jnp.max(logits, axis=1)
    total = jnp.sum(jnp.exp(logits - top[:, None]), axis=1)
    top_all, total_all, target_all = combined_all((top, total, target_logit), "wide", combine_parts)
    log_total = top_all + jnp.log(total_all)
    loss_sum = jnp.sum(weight * (log_total - target_all))
    grad_logits = (jnp.exp(logits - log_total[:, None]) - hits.astype(jnp.float32)) * (
        weight / denominator
    )[:, None]
    grad_logits = grad_logits.astype(jnp.bfloat16)
    grad_unembed = jnp.einsum(
        "rv,rd->vd", grad_logits, gathered, preferred_element_type=jnp.float32
    )
    grad_rows = lax.psum_scatter(
        head_term(grad_logits, table_low[1]), "wide", scatter_dimension=0, tiled=True
    )
    grad_final = jnp.zeros_like(stream).at[mine].add(grad_rows)
    grad_stream, grad_final_gain, grad_final_bias = norm_backward(
        grad_final, final_normal, final_scale, final_gain
    )
    grad_shared = jnp.zeros(shared.shape, jnp.float32)
    collected = [None] * L
    for layer_number in reversed(range(L)):
        grad_stream, grad_shared, collected[layer_number] = layer_backward(
            grad_stream,
            grad_shared,
            layer_vectors[layer_number],
            layer_weights[layer_number],
            kept_all[layer_number],
            shared,
            pair_low,
            setting,
            layer_number == 0,
        )
    grad_embed = embed_add(
        ordered,
        offset,
        jnp.zeros((vocab_rows, D), jnp.float32),
        lax.all_gather(grad_stream, "wide", axis=0, tiled=True),
    )
    grad_tables = jnp.stack([grad_embed, grad_unembed])
    grad_attention = jnp.stack([jnp.stack([piece[0], piece[1]]) for piece in collected])
    grad_feedforward = jnp.stack([jnp.stack([piece[2], piece[3]]) for piece in collected])
    grad_small = jnp.concatenate(
        [piece[6] for piece in collected] + [collected[0][5], grad_final_gain, grad_final_bias]
    )
    return (loss_sum, grad_tables, (grad_attention, grad_feedforward, collected[0][4]), grad_small)


def adam_update(weight, gradient, moment_one, moment_two, clip_factor, step_number, rate):
    gradient = gradient * clip_factor
    moment_one = BETA_ONE * moment_one + (1.0 - BETA_ONE) * gradient
    moment_two = BETA_TWO * moment_two + (1.0 - BETA_TWO) * gradient * gradient
    first_hat = moment_one / (1.0 - BETA_ONE**step_number)
    second_hat = moment_two / (1.0 - BETA_TWO**step_number)
    weight = weight - rate * (first_hat / (jnp.sqrt(second_hat) + ADAM_EPSILON) + DECAY * weight)
    return (weight, moment_one, moment_two)


def add_tuples(former, latter):
    if former is None:
        return latter
    return tuple((left + right for left, right in zip(former, latter)))


def body(
    token_ids,
    prompt_mask,
    loss_pos,
    tables,
    attention,
    feedforward,
    key_value,
    gains_biases,
    first_tables,
    first_attention,
    first_feedforward,
    first_key_value,
    first_gains,
    second_tables,
    second_attention,
    second_feedforward,
    second_key_value,
    second_gains,
    outer_tables,
    outer_attention,
    outer_feedforward,
    outer_key_value,
    outer_gains,
):
    width = lax.axis_size("wide")
    device = lax.axis_index("wide")
    group_total = lax.axis_size("rep")
    masters = (
        lax.all_gather(tables, "rep", axis=2, tiled=True),
        lax.all_gather(attention, "rep", axis=3, tiled=True),
        lax.all_gather(feedforward, "rep", axis=3, tiled=True),
        lax.all_gather(key_value, "rep", axis=1, tiled=True),
        lax.all_gather(gains_biases, "rep", axis=0, tiled=True),
    )
    current = list(masters)
    moment_one = [
        piece[0]
        for piece in (
            first_tables,
            first_attention,
            first_feedforward,
            first_key_value,
            first_gains,
        )
    ]
    moment_two = [
        piece[0]
        for piece in (
            second_tables,
            second_attention,
            second_feedforward,
            second_key_value,
            second_gains,
        )
    ]
    seq_count = token_ids.shape[3]
    rows_seq = LEN // width
    vocab_rows = tables.shape[1]
    bands = width // GROUPS
    band_rows = rows_seq // bands
    places = (device * rows_seq + jnp.arange(rows_seq, dtype=jnp.int32)).astype(jnp.float32)
    cosine_table, sine_table = rotary_tables(jnp.tile(places, seq_count))
    query_places = (
        jnp.arange(width, dtype=jnp.int32)[:, None] * rows_seq
        + device % bands * band_rows
        + jnp.arange(band_rows, dtype=jnp.int32)[None, :]
    ).reshape(-1)
    setting = (cosine_table, sine_table, query_places, seq_count, rows_seq, vocab_rows, device)
    loss_total = jnp.zeros((), jnp.float32)
    table_low = current[0].astype(jnp.bfloat16)
    attention_low = lax.all_gather(current[1].astype(jnp.bfloat16), "wide", axis=2, tiled=True)
    feed_low = lax.all_gather(current[2].astype(jnp.bfloat16), "wide", axis=2, tiled=True)
    pair_low = lax.all_gather(current[3].astype(jnp.bfloat16), "wide", axis=0, tiled=True)
    layer_vectors, pair_bias, final_gain, final_bias = unpack_small(current[4])
    weights_now = (
        table_low,
        attention_low,
        feed_low,
        pair_low,
        layer_vectors,
        pair_bias,
        final_gain,
        final_bias,
    )
    count = jnp.zeros((), jnp.float32)
    for micro_index in range(MICRO):
        seq_index, place_index = loss_rows(loss_pos[0, 0, micro_index], width, rows_seq)
        count = count + jnp.sum(
            prompt_mask[0, 0, micro_index][seq_index, place_index + 1].astype(jnp.float32)
        )
    grad_tables = jnp.zeros(current[0].shape, jnp.float32)
    grad_small = jnp.zeros(current[4].shape, jnp.float32)
    layer_acc = None
    for micro_index in range(MICRO):
        loss_sum, tables_part, layer_part, small_part = micro_pass(
            token_ids[0, 0, micro_index],
            prompt_mask[0, 0, micro_index],
            loss_pos[0, 0, micro_index],
            weights_now,
            setting,
            count,
        )
        loss_total = loss_total + loss_sum
        grad_tables = grad_tables + tables_part
        grad_small = grad_small + small_part
        layer_acc = add_tuples(layer_acc, layer_part)
    layer_shares = (
        lax.psum_scatter(layer_acc[0], "wide", scatter_dimension=2, tiled=True),
        lax.psum_scatter(layer_acc[1], "wide", scatter_dimension=2, tiled=True),
        lax.psum_scatter(layer_acc[2], "wide", scatter_dimension=0, tiled=True),
    )
    squares = jnp.sum(grad_tables * grad_tables)
    for piece in layer_shares:
        squares = squares + jnp.sum(piece * piece)
    small_total, square_total = lax.psum((grad_small, squares), "wide")
    norm = jnp.sqrt(square_total + jnp.sum(small_total * small_total))
    clip_factor = jnp.minimum(1.0, CLIP / (norm + 1e-06))
    gradients = (grad_tables, layer_shares[0], layer_shares[1], layer_shares[2], small_total)
    for index in range(5):
        current[index], moment_one[index], moment_two[index] = adam_update(
            current[index],
            gradients[index],
            moment_one[index],
            moment_two[index],
            clip_factor,
            STEP,
            LEARN_RATES[index],
        )
    differences = tuple((masters[index] - current[index] for index in range(5)))
    averaged = (
        lax.psum_scatter(differences[0], "rep", scatter_dimension=2, tiled=True),
        lax.psum_scatter(differences[1], "rep", scatter_dimension=3, tiled=True),
        lax.psum_scatter(differences[2], "rep", scatter_dimension=3, tiled=True),
        lax.psum_scatter(differences[3], "rep", scatter_dimension=1, tiled=True),
        lax.psum_scatter(differences[4], "rep", scatter_dimension=0, tiled=True),
    )
    initials = (tables, attention, feedforward, key_value, gains_biases)
    outers = (outer_tables, outer_attention, outer_feedforward, outer_key_value, outer_gains)
    new_masters = []
    new_outers = []
    for index in range(5):
        mean_diff = averaged[index] / group_total
        momentum = OUTER_MOMENTUM * outers[index] + mean_diff
        new_outers.append(momentum)
        new_masters.append(initials[index] - OUTER_RATE * (mean_diff + OUTER_MOMENTUM * momentum))
    return (
        loss_total.reshape(1),
        count.reshape(1),
        new_masters[0],
        new_masters[1],
        new_masters[2],
        new_masters[3],
        new_masters[4],
        moment_one[0][None],
        moment_one[1][None],
        moment_one[2][None],
        moment_one[3][None],
        moment_one[4][None],
        moment_two[0][None],
        moment_two[1][None],
        moment_two[2][None],
        moment_two[3][None],
        moment_two[4][None],
        new_outers[0],
        new_outers[1],
        new_outers[2],
        new_outers[3],
        new_outers[4],
    )


def solution(mesh):
    placed = (
        P("rep", None, None, None, None),
        P("rep", None, None, None, None),
        P("rep", None, None, None, None),
        P(None, "wide", "rep"),
        P(None, None, "wide", "rep"),
        P(None, None, "wide", "rep"),
        P("wide", "rep"),
        P("rep"),
        P("rep", None, "wide", None),
        P("rep", None, None, "wide", None),
        P("rep", None, None, "wide", None),
        P("rep", "wide", None),
        P("rep", None),
        P("rep", None, "wide", None),
        P("rep", None, None, "wide", None),
        P("rep", None, None, "wide", None),
        P("rep", "wide", None),
        P("rep", None),
        P(None, "wide", "rep"),
        P(None, None, "wide", "rep"),
        P(None, None, "wide", "rep"),
        P("wide", "rep"),
        P("rep"),
    )
    return jax.shard_map(
        body,
        mesh=mesh,
        in_specs=placed,
        out_specs=(
            P("rep"),
            P("rep"),
            P(None, "wide", "rep"),
            P(None, None, "wide", "rep"),
            P(None, None, "wide", "rep"),
            P("wide", "rep"),
            P("rep"),
            P("rep", None, "wide", None),
            P("rep", None, None, "wide", None),
            P("rep", None, None, "wide", None),
            P("rep", "wide", None),
            P("rep", None),
            P("rep", None, "wide", None),
            P("rep", None, None, "wide", None),
            P("rep", None, None, "wide", None),
            P("rep", "wide", None),
            P("rep", None),
            P(None, "wide", "rep"),
            P(None, None, "wide", "rep"),
            P(None, None, "wide", "rep"),
            P("wide", "rep"),
            P("rep"),
        ),
        check_vma=False,
    )
```

profile of v0, /device:TPU:0, one launch (start us, length us, event | category | flops | bytes accessed | tf_op | source)
XLA Modules:
  0.0 1921.1 jit_solution(11521238013655615158)
XLA Ops:
  9.5 235.5 %all-gather.19.cloned.1.call-done = f32[2,6288,512]{2,1,0:T(8,128)} async-done(((f32[2,6288,128]{2,1,0:T(8,128)}), f32[2,6288,512]{2,1,0:T(8,128)}) %all-gather.19.cloned.1.call-update) | async-done | bytes 25755664 | tf_op jit(solution)/shard_map/all_gather | solution.py:470
  245.0 9.4 convert_element_type.480
  262.3 11.2 gather_fusion.1
  275.3 11.2 gather_fusion.5
  289.1 13.3 all_gather.83
  308.6 16.0 all-reduce
  339.1 15.0 all_gather.81
  368.5 20.1 %all-gather.21.cloned.1.call-done = bf16[2,2,512,512]{3,2,1,0:T(8,128)(2,1)} async-done(((bf16[2,2,64,512]{3,2,1,0:T(8,128)(2,1)}), bf16[2,2,512,512]{3,2,1,0:T(8,128)(2,1)}) %all-gather.21.cloned.1.call-update) | async-done | bytes 2097168 | tf_op jit(solution)/shard_map/all_gather | solution.py:512
  404.7 73.0 %all-gather.25.cloned.1.call-done = bf16[2,2,512,2048]{3,2,1,0:T(8,128)(2,1)} async-done(((bf16[2,2,64,2048]{3,2,1,0:T(8,128)(2,1)}), bf16[2,2,512,2048]{3,2,1,0:T(8,128)(2,1)}) %all-gather.25.cloned.1.call-update) | async-done | bytes 8388624 | tf_op jit(solution)/shard_map/all_gather | solution.py:513
  493.5 15.8 all_gather.82
  509.3 16.3 all_gather.94
  529.4 9.3 fusion.325
  538.7 8.0 fusion.35
  562.3 9.3 fusion.323
  620.3 8.1 multiply_convert_fusion.4
  648.7 9.2 fusion.329
  682.7 8.9 fusion.327
  729.8 14.1 all_gather.95
  749.6 9.6 all-gather.11
  759.2 9.1 all-gather.10
  768.3 9.6 all-gather.9
  779.9 14.0 all_gather.87
  801.1 9.1 all-gather.7
  810.2 9.6 all-gather.8
  819.7 9.1 all-gather.6
  845.4 24.3 %reduce-scatter.20.cloned.1.call-done = f32[16,512]{1,0:T(8,128)} async-done(((f32[128,512]{1,0:T(8,128)}), f32[16,512]{1,0:T(8,128)}) %reduce-scatter.20.cloned.1.call-update) | async-done | bytes 32784 | tf_op jit(solution)/shard_map/reduce_scatter | solution.py:389
  872.9 28.3 %reduce-scatter.24.cloned.1.call-done = f32[16,512]{1,0:T(8,128)} async-done(((f32[128,512]{1,0:T(8,128)}), f32[16,512]{1,0:T(8,128)}) %reduce-scatter.24.cloned.1.call-update) | async-done | bytes 32784 | tf_op jit(solution)/shard_map/reduce_scatter | solution.py:389
  934.8 13.4 fusion.26
  948.2 10.1 fusion.83
  972.4 13.8 fusion.32
  986.2 9.7 fusion.77
  1052.9 13.4 fusion.29
  1066.3 10.1 fusion.80
  1129.8 13.0 fusion.23
  1142.8 12.2 fusion.25
  1263.8 12.5 maximum_add_fusion.2
  1300.1 27.0 %all-gather.29.cloned.1.call-done = f32[2048,512]{1,0:T(8,128)} async-done(((f32[256,512]{1,0:T(8,128)}), f32[2048,512]{1,0:T(8,128)}) %all-gather.29.cloned.1.call-update) | async-done | bytes 4194320 | tf_op jit(solution)/shard_map/all_gather | solution.py:414
  1327.1 21.0 %scatter_custom_fusion.3 = f32[6288,512]{1,0:T(8,128)} fusion(s32[2048]{0:T(1024)} %bitcast.908, f32[]{:T(128)} %constant.451.clone.1, f32[2048,512]{1,0:T(8,128)} %all-gather.29.cloned.1.call-done, pred[2048]{0:T(1024)(128)(4,1)S(1)} %copy-done.171), kind=kCustom, calls=%fused_computation.115 | custom fusion | flops 2097152 | bytes 17075200 | tf_op jit(solution)/shard_map/scatter-add | solution.py:315
  1348.1 27.0 %all-gather.27.cloned.1.call-done = f32[2048,512]{1,0:T(8,128)} async-done(((f32[256,512]{1,0:T(8,128)}), f32[2048,512]{1,0:T(8,128)}) %all-gather.27.cloned.1.call-update) | async-done | bytes 4194320 | tf_op jit(solution)/shard_map/all_gather | solution.py:414
  1375.1 20.6 %scatter_custom_fusion.1 = f32[6288,512]{1,0:T(8,128)} fusion(s32[2048]{0:T(1024)} %bitcast.906, f32[]{:T(128)} %constant.451.clone.1, f32[2048,512]{1,0:T(8,128)} %all-gather.27.cloned.1.call-done, pred[2048]{0:T(1024)(128)(4,1)S(1)} %copy-done.169), kind=kCustom, calls=%fused_computation.117 | custom fusion | flops 2097152 | bytes 17075200 | tf_op jit(solution)/shard_map/scatter-add | solution.py:315
  1395.7 18.2 multiply_reduce_fusion
  1415.3 129.7 %reduce-scatter.30.cloned.1.call-done = f32[2,2,64,2048]{3,2,1,0:T(8,128)} async-done(((f32[2,2,512,2048]{3,2,1,0:T(8,128)}), f32[2,2,64,2048]{3,2,1,0:T(8,128)}) %reduce-scatter.30.cloned.1.call-update) | async-done | bytes 2097168 | tf_op jit(solution)/shard_map/reduce_scatter | solution.py:550
  1549.0 26.4 %all-reduce.2 = (f32[]{:T(128)}, f32[12416]{0:T(1024)S(1)}) all-reduce(f32[]{:T(128)S(6)} %add.1180, f32[12416]{0:T(1024)S(1)} %add.1181), channel_id=1, replica_groups=mesh['rep'=4,'wide'=8] {'wide'}, use_global_device_ids=true, to_apply=%region_75.76 | all-reduce | flops 12417 | bytes 99336 | tf_op jit(solution)/shard_map/psum | solution.py:556
  1589.4 51.3 %subtract_subtract_fusion = f32[2,6288,512]{2,1,0:T(8,128)} fusion(f32[2,6288,512]{2,1,0:T(8,128)} %all-gather.19.cloned.1.call-done, f32[1,2,6288,512]{3,2,1,0:T(8,128)} %param.40, f32[1,2,6288,512]{3,2,1,0:T(8,128)} %param.35, f32[]{:T(128)S(6)} %min_shard_map.3, f32[1,6288,512]{2,1,0:T(8,128)} %bitcast.828, f32[1,6288,512]{2,1,0:T(8,128)} %bitcast.831, ...), kind=kLoop, calls=%fused_computation.33 | loop fusion | flops 128778240 | bytes 154533888 | tf_op jit(solution)/shard_map/sub | solution.py:570
  1645.2 17.5 all-reduce.1
  1663.5 54.0 %fusion.20 = (f32[1,2,6288,512]{3,2,1,0:T(8,128)}, f32[1,2,6288,512]{3,2,1,0:T(8,128)}) fusion(f32[1,2,6288,512]{3,2,1,0:T(8,128)} %param.40, f32[]{:T(128)S(6)} %min_shard_map.3, f32[1,1,6288,512]{3,2,1,0:T(8,128)} %bitcast.829, f32[1,1,6288,512]{3,2,1,0:T(8,128)} %bitcast.832, f32[1,1,6288,512]{3,2,1,0:T(8,128)} %bitcast.826, ...), kind=kLoop, calls=%fused_computation.41 | loop fusion | flops 70828032 | bytes 154533888 | tf_op jit(solution)/shard_map/add | solution.py:428
  1723.5 176.2 %reduce-scatter.34.cloned.1.call-done = f32[2,6288,128]{2,1,0:T(8,128)} async-done(((f32[2,6288,512]{2,1,0:T(8,128)}), f32[2,6288,128]{2,1,0:T(8,128)}) %reduce-scatter.34.cloned.1.call-update) | async-done | bytes 6438928 | tf_op jit(solution)/shard_map/reduce_scatter | solution.py:572
  1899.7 12.4 multiply_subtract_fusion
  (968 shorter events, 577.1 us)
Async XLA Ops:
  7.2 237.8 %all-gather.19.cloned.1.call-start = ((), (), s32[]{:S(2)}) async-start(), calls=%async_computation.29 | async-start | bytes 32194560 | tf_op jit(solution)/shard_map/all_gather | solution.py:470
  7.9 296.2 %all-gather.23.cloned.1.call-start = ((), (), s32[]{:S(2)}) async-start(), calls=%async_computation.32 | async-start | bytes 2621440 | tf_op jit(solution)/shard_map/all_gather | solution.py:472
  8.7 352.4 %reduce-scatter.16.cloned.1.call-start = ((), (), s32[]{:S(2)}) async-start(), calls=%async_computation.30 | async-start | bytes 2359296 | tf_op jit(solution)/shard_map/reduce_scatter | solution.py:345
  8.8 264.7 %copy-start.168 = (pred[2048]{0:T(1024)(128)(4,1)}, pred[2048]{0:T(1024)(128)(4,1)S(1)}, u32[]{:S(2)}) copy-start(pred[2048]{0:T(1024)(128)(4,1)S(1)} %get-tuple-element.743) | copy-start | bytes 6148
  8.8 277.7 %copy-start.170 = (pred[2048]{0:T(1024)(128)(4,1)}, pred[2048]{0:T(1024)(128)(4,1)S(1)}, u32[]{:S(2)}) copy-start(pred[2048]{0:T(1024)(128)(4,1)S(1)} %get-tuple-element.742) | copy-start | bytes 6148
  8.9 266.4 %copy-start.155 = (s32[2048,1]{0,1:T(1,128)}, s32[2048,1]{0,1:T(1,128)S(1)}, u32[]{:S(2)}) copy-start(s32[2048,1]{0,1:T(1,128)S(1)} %get-tuple-element.894) | copy-start | bytes 24580
  275.2 89.6 %reduce-scatter.18.cloned.1.call-start = ((), (), s32[]{:S(2)}) async-start(), calls=%async_computation.34 | async-start | bytes 2359296 | tf_op jit(solution)/shard_map/reduce_scatter | solution.py:345
  288.2 100.3 %all-gather.21.cloned.1.call-start = ((), (), s32[]{:S(2)}) async-start(), calls=%async_computation.31 | async-start | bytes 2359296 | tf_op jit(solution)/shard_map/all_gather | solution.py:512
  304.1 173.6 %all-gather.25.cloned.1.call-start = ((), (), s32[]{:S(2)}) async-start(), calls=%async_computation.33 | async-start | bytes 9437184 | tf_op jit(solution)/shard_map/all_gather | solution.py:513
  357.3 253.9 %copy-start.105 = (f32[256,8]{0,1:T(8,128)}, f32[256,8]{0,1:T(8,128)S(1)}, u32[]{:S(2)}) copy-start(f32[256,8]{0,1:T(8,128)S(1)} %get-tuple-element.917) | copy-start | bytes 24580
  358.0 250.1 %copy-start.134 = (f32[512]{0:T(512)}, f32[512]{0:T(512)S(1)}, u32[]{:S(2)}) copy-start(f32[512]{0:T(512)S(1)} %get-tuple-element.876) | copy-start | bytes 6148
  358.0 250.1 %copy-start.176 = (f32[512]{0:T(512)}, f32[512]{0:T(512)S(1)}, u32[]{:S(2)}) copy-start(f32[512]{0:T(512)S(1)} %get-tuple-element.875) | copy-start | bytes 6148
  358.0 270.4 %copy-start.111 = (f32[512]{0:T(512)}, f32[512]{0:T(512)S(1)}, u32[]{:S(2)}) copy-start(f32[512]{0:T(512)S(1)} %get-tuple-element.872) | copy-start | bytes 6148
  358.0 270.3 %copy-start.115 = (f32[512]{0:T(512)}, f32[512]{0:T(512)S(1)}, u32[]{:S(2)}) copy-start(f32[512]{0:T(512)S(1)} %get-tuple-element.871) | copy-start | bytes 6148
  398.5 127.2 %all-to-all-start = ((bf16[8,1,128,128]{3,2,1,0:T(8,128)(2,1)}), bf16[8,1,128,128]{3,2,1,0:T(8,128)(2,1)S(1)}, u32[]{:S(2)}, u32[]{:S(2)}) async-start(bf16[8,1,128,128]{3,2,1,0:T(8,128)(2,1)} %bitcast.23), calls=%async_computation.1 | async-start | bytes 524288 | tf_op jit(solution)/shard_map/all_to_all | solution.py:95
  525.7 29.4 %all-to-all-start.4 = ((bf16[8,1,128,128]{3,2,1,0:T(8,128)(2,1)}), bf16[8,1,128,128]{3,2,1,0:T(8,128)(2,1)S(1)}, u32[]{:S(2)}, u32[]{:S(2)}) async-start(bf16[8,1,128,128]{3,2,1,0:T(8,128)(2,1)} %bitcast.71), calls=%async_computation.6 | async-start | bytes 524288 | tf_op jit(solution)/shard_map/all_to_all | solution.py:95
  555.1 34.1 %all-to-all-start.1 = ((bf16[8,1,128,128]{3,2,1,0:T(8,128)(2,1)}), bf16[8,1,128,128]{3,2,1,0:T(8,128)(2,1)S(1)}, u32[]{:S(2)}, u32[]{:S(2)}) async-start(bf16[8,1,128,128]{3,2,1,0:T(8,128)(2,1)} %copy.313), calls=%async_computation.2 | async-start | bytes 524288 | tf_op jit(solution)/shard_map/all_to_all | solution.py:99
  589.2 14.9 all-to-all-start.5
  615.8 25.8 %all-to-all-start.2 = ((bf16[8,1,128,128]{3,2,1,0:T(8,128)(2,1)}), bf16[8,1,128,128]{3,2,1,0:T(8,128)(2,1)S(1)}, u32[]{:S(2)}, u32[]{:S(2)}) async-start(bf16[8,1,128,128]{3,2,1,0:T(8,128)(2,1)} %bitcast.886), calls=%async_computation.3 | async-start | bytes 524288 | tf_op jit(solution)/shard_map/all_to_all | solution.py:95
  641.6 32.6 %all-to-all-start.6 = ((bf16[8,1,128,128]{3,2,1,0:T(8,128)(2,1)}), bf16[8,1,128,128]{3,2,1,0:T(8,128)(2,1)}, u32[]{:S(2)}, u32[]{:S(2)}) async-start(bf16[8,1,128,128]{3,2,1,0:T(8,128)(2,1)} %bitcast.887), calls=%async_computation.8 | async-start | bytes 524288 | tf_op jit(solution)/shard_map/all_to_all | solution.py:95
  674.2 33.8 %all-to-all-start.3 = ((bf16[8,1,128,128]{3,2,1,0:T(8,128)(2,1)}), bf16[8,1,128,128]{3,2,1,0:T(8,128)(2,1)}, u32[]{:S(2)}, u32[]{:S(2)}) async-start(bf16[8,1,128,128]{3,2,1,0:T(8,128)(2,1)} %copy.320), calls=%async_computation.4 | async-start | bytes 524288 | tf_op jit(solution)/shard_map/all_to_all | solution.py:99
  708.0 15.0 all-to-all-start.7
  713.1 156.6 %reduce-scatter.20.cloned.1.call-start = ((), (), s32[]{:S(2)}) async-start(), calls=%async_computation.35 | async-start | bytes 294912 | tf_op jit(solution)/shard_map/reduce_scatter | solution.py:389
  840.3 60.9 %reduce-scatter.24.cloned.1.call-start = ((), (), s32[]{:S(2)}) async-start(), calls=%async_computation.38 | async-start | bytes 294912 | tf_op jit(solution)/shard_map/reduce_scatter | solution.py:389
  915.5 14.0 all-to-all-start.12
  929.5 41.7 %all-to-all-start.8 = ((bf16[8,1,128,128]{3,2,1,0:T(8,128)(2,1)}), bf16[8,1,128,128]{3,2,1,0:T(8,128)(2,1)}, u32[]{:S(2)}, u32[]{:S(2)}) async-start(bf16[8,1,128,128]{3,2,1,0:T(8,128)(2,1)} %bitcast.103), calls=%async_computation.11 | async-start | bytes 524288 | tf_op jit(solution)/shard_map/all_to_all | solution.py:95
  1007.9 14.8 all-to-all-start.9
  1022.7 13.8 all-to-all-start.13
  1036.6 15.0 all-to-all-start.10
  1088.6 13.1 all-to-all-start.11
  1114.7 13.8 all-to-all-start.14
  1118.8 70.8 %reduce-scatter.22.cloned.1.call-start = ((), (), s32[]{:S(2)}) async-start(), calls=%async_computation.36 | async-start | bytes 1179648 | tf_op jit(solution)/shard_map/reduce_scatter | solution.py:266
  1121.2 73.5 %reduce-scatter.26.cloned.1.call-start = ((), (), s32[]{:S(2)}) async-start(), calls=%async_computation.39 | async-start | bytes 1179648 | tf_op jit(solution)/shard_map/reduce_scatter | solution.py:266
  1171.5 16.5 all-to-all-start.15
  1174.9 122.1 %reduce-scatter.32.cloned.1.call-start = ((), (), s32[]{:S(2)}) async-start(), calls=%async_computation.43 | async-start | bytes 294912 | tf_op jit(solution)/shard_map/reduce_scatter | solution.py:551
  1199.5 98.8 %reduce-scatter.28.cloned.1.call-start = ((), (), s32[]{:S(2)}) async-start(), calls=%async_computation.41 | async-start | bytes 4718592 | tf_op jit(solution)/shard_map/reduce_scatter | solution.py:549
  1208.1 119.1 %all-gather.29.cloned.1.call-start = ((), (), s32[]{:S(2)}) async-start(), calls=%async_computation.40 | async-start | bytes 4718592 | tf_op jit(solution)/shard_map/all_gather | solution.py:414
  1228.4 146.7 %all-gather.27.cloned.1.call-start = ((), (), s32[]{:S(2)}) async-start(), calls=%async_computation.37 | async-start | bytes 4718592 | tf_op jit(solution)/shard_map/all_gather | solution.py:414
  1229.0 316.0 %reduce-scatter.30.cloned.1.call-start = ((), (), s32[]{:S(2)}) async-start(), calls=%async_computation.42 | async-start | bytes 18874368 | tf_op jit(solution)/shard_map/reduce_scatter | solution.py:550
  1276.4 441.1 %reduce-scatter.40.cloned.1.call-start = ((), (), s32[]{:S(2)}) async-start(), calls=%async_computation.47 | async-start | bytes 81920
  1413.9 163.5 %copy-start.119 = (f32[64,128]{1,0:T(8,128)S(1)}, f32[64,128]{1,0:T(8,128)}, u32[]{:S(2)}) copy-start(f32[64,128]{1,0:T(8,128)} %reduce-scatter.32.cloned.1.call-done) | copy-start | bytes 98308
  1413.9 163.5 %copy-start.151 = (f32[1,64,128]{2,1,0:T(8,128)S(1)}, f32[1,64,128]{2,1,0:T(8,128)}, u32[]{:S(2)}) copy-start(f32[1,64,128]{2,1,0:T(8,128)} %param.43) | copy-start | bytes 98308
  1413.9 163.5 %copy-start.152 = (f32[1,64,128]{2,1,0:T(8,128)S(1)}, f32[1,64,128]{2,1,0:T(8,128)}, u32[]{:S(2)}) copy-start(f32[1,64,128]{2,1,0:T(8,128)} %param.38) | copy-start | bytes 98308
  1413.9 165.0 %copy-start.34 = (f32[2,2,64,512]{3,2,1,0:T(8,128)S(1)}, f32[2,2,64,512]{3,2,1,0:T(8,128)}, u32[]{:S(2)}) copy-start(f32[2,2,64,512]{3,2,1,0:T(8,128)} %copy-done.33) | copy-start | bytes 1572868
  1413.9 165.0 %copy-start.64 = (f32[2,2,64,512]{3,2,1,0:T(8,128)S(1)}, f32[2,2,64,512]{3,2,1,0:T(8,128)}, u32[]{:S(2)}) copy-start(f32[2,2,64,512]{3,2,1,0:T(8,128)} %reduce-scatter.28.cloned.1.call-done) | copy-start | bytes 1572868
  1578.9 140.8 %reduce-scatter.36.cloned.1.call-start = ((), (), s32[]{:S(2)}) async-start(), calls=%async_computation.45 | async-start | bytes 655360 | tf_op jit(solution)/shard_map/reduce_scatter | solution.py:573
  1581.8 139.5 %reduce-scatter.38.cloned.1.call-start = ((), (), s32[]{:S(2)}) async-start(), calls=%async_computation.46 | async-start | bytes 2621440 | tf_op jit(solution)/shard_map/reduce_scatter | solution.py:574
  1589.2 310.5 %reduce-scatter.34.cloned.1.call-start = ((), (), s32[]{:S(2)}) async-start(), calls=%async_computation.44 | async-start | bytes 32194560 | tf_op jit(solution)/shard_map/reduce_scatter | solution.py:572
  (232 other events, 3585.7 us)
Sparse Core Ops, SparseCore 0:
  9.9 235.1 all-gather.18
  246.9 35.3 all-gather.22
  285.1 35.7 reduce-scatter.15
  323.6 34.8 reduce-scatter.17
  360.6 27.9 all-gather.20
  390.6 87.0 all-gather.24
  840.4 29.2 reduce-scatter.19
  872.6 28.4 reduce-scatter.23
  1121.9 33.5 reduce-scatter.21
  1162.5 32.1 reduce-scatter.25
  1199.7 28.8 reduce-scatter.31
  1231.4 48.1 reduce-scatter.27
  1281.8 45.2 all-gather.28
  1329.2 45.8 all-gather.26
  1378.0 166.9 reduce-scatter.29
  1579.0 21.8 reduce-scatter.39
  1604.1 24.7 reduce-scatter.35
  1632.6 36.6 reduce-scatter.37
  1672.4 227.2 reduce-scatter.33
where the time goes:
time: 1930 us; the launch traced here: 1920 us
  waiting for transfers between devices  774 us (40%)
  other arithmetic  373 us (19%)
  matrix products  340 us (18%)
  blocking collectives  212 us (11%)
  local copies, waits for them, and re-layouts  121 us (6%)
  starting transfers between devices  72.2 us (4%)
  between operations  28.6 us (1%)
    all_gather x1, waiting for transfers between devices, body(): lax.all_gather(tables, 'rep', axis=2, tiled=True)  236 us
    reduce_scatter x1, waiting for transfers between devices, body(): lax.psum_scatter(differences[0], 'rep', scatter_dimension=2, tiled=True)  176 us
    reduce_scatter x1, waiting for transfers between devices, body(): lax.psum_scatter(layer_acc[1], 'wide', scatter_dimension=2, tiled=True)  130 us
    all_gather x1, waiting for transfers between devices, body(): lax.all_gather(current[2].astype(jnp.bfloat16), 'wide', axis=2, tiled=True)  73 us
    all_gather x6, blocking collectives, combined_all(): everything = jax.tree.map(lambda part: lax.all_gather(part, axis), value)  56 us
    add x1, other arithmetic, adam_update(): moment_two = BETA_TWO * moment_two + (1.0 - BETA_TWO) * gradient * gradient  54 us
    all_gather x2, waiting for transfers between devices, micro_pass(): lax.all_gather(grad_stream, 'wide', axis=0, tiled=True)  54 us
    dot_general x4, matrix products, attend_backward(): jnp.einsum('qhd,kd->hqk', grad_context, pairs[:, HD:], preferred_element_...  53.5 us
  transfers between devices with their start and end apart: 35, of which 17 were waited for; matrix products, arithmetic and copies ran while one was open for 34% of the time, Pallas kernels for 0%

commit v1 on v0

v1 whole, which is shorter than its diff:
```python
from functools import partial

import jax
import jax.numpy as jnp
from jax import lax
from jax.sharding import PartitionSpec as P

D = 512
HEADS = 8
HD = 64
ROT = 16
FF = 2048
L = 2
LEN = 2048
MICRO = 2
STEP = 5

NORM_EPSILON = 1e-05
CLIP = 0.1
LEARN_RATES = (0.02, 0.2, 0.02, 0.02, 0.2)
BETA_ONE = 0.9
BETA_TWO = 0.95
ADAM_EPSILON = 1e-08
DECAY = 0.1
OUTER_RATE = 0.7
OUTER_MOMENTUM = 0.9
FIX_ONE = 1.0 / (1.0 - BETA_ONE**STEP)
FIX_TWO = 1.0 / (1.0 - BETA_TWO**STEP)

BF = jnp.bfloat16
F4 = jnp.float32


def dot(left, right, dims):
    return lax.dot_general(left, right, (dims, ((), ())), preferred_element_type=F4)


def normal_of(stream):
    centred = stream - jnp.mean(stream, axis=-1, keepdims=True)
    scale = lax.rsqrt(jnp.mean(centred * centred, axis=-1, keepdims=True) + NORM_EPSILON)
    return centred * scale, scale


def norm_pull(shaped, normal, scale):
    return scale * (
        shaped
        - jnp.mean(shaped, axis=-1, keepdims=True)
        - normal * jnp.mean(shaped * normal, axis=-1, keepdims=True)
    )


def rotary(places):
    frequency = 10000.0 ** (-2.0 * jnp.arange(ROT // 2, dtype=F4) / ROT)
    angles = places.astype(F4)[:, None] * frequency[None, :]
    return jnp.cos(angles), jnp.sin(angles)


def rotate(values, cosine, sine):
    half = ROT // 2
    a = values[..., :half]
    b = values[..., half:ROT]
    c = cosine[:, None, :]
    s = sine[:, None, :]
    return jnp.concatenate([a * c - b * s, b * c + a * s, values[..., ROT:]], axis=-1)


def unpack_small(gains_biases):
    span = 7 * D + FF
    layers = gains_biases[: L * span].reshape(L, span)
    remain = gains_biases[L * span :]
    return layers, remain[: 2 * HD], remain[2 * HD : 2 * HD + D], remain[2 * HD + D :]


def moments_step(gradient, one, two):
    one = BETA_ONE * one + (1.0 - BETA_ONE) * gradient
    two = BETA_TWO * two + (1.0 - BETA_TWO) * gradient * gradient
    return one, two, (one * FIX_ONE) / (jnp.sqrt(two * FIX_TWO) + ADAM_EPSILON)


def attend_forward(queries, keys, values, allowed):
    def head(query):
        scores = jnp.einsum("mnd,mkd->mnk", query, keys, preferred_element_type=F4) * 0.125
        scores = jnp.where(allowed, scores, -1e30)
        top = jnp.max(scores, axis=2, keepdims=True)
        expo = jnp.exp(scores - top)
        total = jnp.sum(expo, axis=2, keepdims=True)
        probs = (expo / total).astype(BF)
        context = jnp.einsum("mnk,mkd->mnd", probs, values, preferred_element_type=F4)
        return context.astype(BF), top + jnp.log(total)

    context, log_total = lax.map(head, queries.transpose(2, 0, 1, 3))
    return context.transpose(1, 2, 0, 3), log_total


def attend_backward(queries, keys, values, allowed, log_total, grad_context):
    def head(so_far, inputs):
        query, logs, grad = inputs
        scores = jnp.einsum("mnd,mkd->mnk", query, keys, preferred_element_type=F4) * 0.125
        scores = jnp.where(allowed, scores, -1e30)
        probs = jnp.exp(scores - logs)
        grad_probs = jnp.einsum("mnd,mkd->mnk", grad, values, preferred_element_type=F4)
        inner = jnp.sum(probs * grad_probs, axis=2, keepdims=True)
        grad_scores = (probs * (grad_probs - inner)).astype(BF)
        grad_query = jnp.einsum("mnk,mkd->mnd", grad_scores, keys, preferred_element_type=F4)
        grad_keys = jnp.einsum("mnk,mnd->mkd", grad_scores, query, preferred_element_type=F4)
        grad_values = jnp.einsum(
            "mnk,mnd->mkd", probs.astype(BF), grad, preferred_element_type=F4
        )
        both = jnp.concatenate([grad_keys * 0.125, grad_values], axis=-1)
        return so_far + both, (grad_query * 0.125).astype(BF)

    start = jnp.zeros(keys.shape[:2] + (2 * HD,), F4)
    total, grad_queries = lax.scan(
        head, start, (queries.transpose(2, 0, 1, 3), log_total, grad_context.transpose(2, 0, 1, 3))
    )
    return grad_queries.transpose(1, 2, 0, 3), total


def body(
    token_ids,
    prompt_mask,
    loss_pos,
    tables,
    attention,
    feedforward,
    key_value,
    gains_biases,
    first_tables,
    first_attention,
    first_feedforward,
    first_key_value,
    first_gains,
    second_tables,
    second_attention,
    second_feedforward,
    second_key_value,
    second_gains,
    outer_tables,
    outer_attention,
    outer_feedforward,
    outer_key_value,
    outer_gains,
):
    width = lax.axis_size("wide")
    reps = lax.axis_size("rep")
    w = lax.axis_index("wide")
    seqs = token_ids.shape[3]
    rows_seq = LEN // width
    block = seqs * rows_seq
    cap = 2 * block // width
    vr = tables.shape[1]
    lrows = loss_pos.shape[4]
    n_loss = MICRO * width * lrows
    n_slots = MICRO * width * cap
    swap = [(i, i ^ 1) for i in range(width)]

    base_one = BETA_ONE * first_tables[0, 0]
    base_two = BETA_TWO * second_tables[0, 0]
    base_step = (base_one * FIX_ONE) / (jnp.sqrt(base_two * FIX_TWO) + ADAM_EPSILON)
    base_sum = lax.psum_scatter(
        base_step.astype(BF).reshape(vr, reps, D // reps).transpose(1, 0, 2),
        "rep",
        scatter_dimension=0,
        tiled=True,
    )[0]

    att_low = lax.all_gather(attention.astype(BF), "rep", axis=0)
    ff_low = lax.all_gather(feedforward.astype(BF), "rep", axis=0)
    kv_low = lax.all_gather(key_value.astype(BF), "rep", axis=1, tiled=True)
    att_low = lax.all_gather(att_low, "wide", axis=3, tiled=True)
    ff_low = lax.all_gather(ff_low, "wide", axis=3, tiled=True)
    kv_low = lax.all_gather(kv_low, "wide", axis=0, tiled=True)
    att_low = att_low.transpose(1, 2, 3, 0, 4).reshape(L, 2, D, D)
    ff_low = ff_low.transpose(1, 2, 3, 0, 4).reshape(L, 2, D, FF)
    unembed = lax.all_gather(tables[1].astype(BF), "rep", axis=1, tiled=True)
    small = lax.all_gather(gains_biases, "rep", axis=0, tiled=True)
    vectors, pair_bias, final_gain, final_bias = unpack_small(small)

    tokens_all = lax.all_gather(token_ids[0, 0], "rep")
    ordered_all = tokens_all.reshape(reps, MICRO, seqs, width, rows_seq).transpose(0, 1, 3, 2, 4)
    ordered_all = ordered_all.reshape(reps, MICRO, width, block)
    lower = (jnp.arange(block)[:, None] <= jnp.arange(block)[None, :]).astype(BF)

    def slots_of(labels_hit, payload):
        rank = jnp.einsum("...t,ts->...s", labels_hit.astype(BF), lower, preferred_element_type=F4)
        rank = rank.astype(jnp.int32) - 1
        hot = labels_hit[..., None] & (rank[..., None] == jnp.arange(cap, dtype=jnp.int32))
        valid = rank[..., -1:] >= jnp.arange(cap, dtype=jnp.int32)
        return jnp.sum(jnp.where(hot, payload[..., None], 0), axis=-2), valid

    local_all = ordered_all - w * vr
    slot_ids, slot_valid = slots_of((local_all >= 0) & (local_all < vr), local_all)
    slot_ids = slot_ids.reshape(reps, n_slots)
    slot_valid = slot_valid.reshape(reps, n_slots)

    mine_ordered = lax.dynamic_index_in_dim(ordered_all, lax.axis_index("rep"), 0, False)
    place_codes = (
        jnp.arange(seqs, dtype=jnp.int32)[None, :, None] * LEN
        + jnp.arange(width, dtype=jnp.int32)[:, None, None] * rows_seq
        + jnp.arange(rows_seq, dtype=jnp.int32)[None, None, :]
    ).reshape(width, block)
    shard_hit = (mine_ordered // vr)[None] == jnp.arange(width, dtype=jnp.int32)[
        :, None, None, None
    ]
    key_codes, key_valid = slots_of(
        shard_hit, jnp.broadcast_to(place_codes[None, None], shard_hit.shape)
    )
    key_codes = jnp.where(key_valid, key_codes, seqs * LEN)
    own_codes = lax.dynamic_index_in_dim(key_codes, w, 0, False)
    key_codes = key_codes.transpose(1, 0, 2, 3).reshape(MICRO, width * width * cap)

    rows = jnp.take(tables[0], slot_ids.reshape(-1), axis=0).astype(BF)
    rows = rows.reshape(reps, n_slots, D // reps)
    rows = lax.all_to_all(rows, "rep", 0, 0, tiled=True)
    rows = rows.transpose(1, 0, 2).reshape(n_slots, D)

    slot_normal, slot_scale = normal_of(rows.astype(F4))
    gain0, bias0 = vectors[0, :D], vectors[0, D : 2 * D]
    slot_normed = (slot_normal * gain0 + bias0).astype(BF)
    projected = dot(slot_normed, kv_low, ((1,), (0,))) + pair_bias
    slot_cos, slot_sin = rotary(own_codes.reshape(-1) % LEN)
    turned = rotate(projected[:, None, :HD], slot_cos, slot_sin)[:, 0]
    pairs = jnp.concatenate([turned, projected[:, HD:]], axis=1).astype(BF)
    pairs_all = lax.all_gather(pairs.reshape(MICRO, width * cap, 2 * HD), "wide", axis=1)
    pairs_all = pairs_all.reshape(MICRO, width * width * cap, 2 * HD)
    keys, values = pairs_all[..., :HD], pairs_all[..., HD:]

    codes = loss_pos[0, 0]
    row_seq = codes // (rows_seq - 1)
    row_place = jnp.arange(width, dtype=jnp.int32)[:, None] * rows_seq + codes % (rows_seq - 1)
    row_code = (row_seq * LEN + row_place).reshape(MICRO, width * lrows)
    row_pos = row_place.reshape(-1)
    flat_tokens = token_ids[0, 0].reshape(MICRO, seqs * LEN)
    flat_mask = prompt_mask[0, 0].reshape(MICRO, seqs * LEN)
    targets = jnp.take_along_axis(flat_tokens, row_code + 1, axis=1).reshape(-1)
    weight = jnp.take_along_axis(flat_mask, row_code + 1, axis=1).reshape(-1).astype(F4)
    count = jnp.sum(weight)
    own_micro = own_codes.reshape(MICRO, width * cap)
    pick = jnp.concatenate(
        [
            jnp.concatenate(
                [
                    (row_code[m][:, None] == own_micro[n][None, :])
                    if m == n
                    else jnp.zeros((width * lrows, width * cap), bool)
                    for n in range(MICRO)
                ],
                axis=1,
            )
            for m in range(MICRO)
        ],
        axis=0,
    ).astype(BF)
    picked_rows = dot(pick, rows, ((1,), (0,)))
    stream = lax.psum(picked_rows, "wide")

    allowed = (key_codes[:, None, :] <= row_code[:, :, None]) & (
        key_codes[:, None, :] >= (row_code // LEN * LEN)[:, :, None]
    )
    row_cos, row_sin = rotary(row_pos)
    parity = w % 2
    half = D // 2

    def half_of(array):
        return lax.dynamic_slice_in_dim(array, parity * half, half, axis=1)

    def join(part):
        other = lax.ppermute(part, "wide", swap)
        low_part = jnp.where(parity == 0, part, other)
        high_part = jnp.where(parity == 0, other, part)
        return jnp.concatenate([low_part, high_part], axis=1)

    def heads_of(array):
        return half_of(array).reshape(MICRO, width * lrows, HEADS // 2, HD)

    kept = []
    for k in range(L):
        vec = vectors[k]
        normal, scale = normal_of(stream)
        normed = (normal * vec[:D] + vec[D : 2 * D]).astype(BF)
        feed = (normal * vec[2 * D : 3 * D] + vec[3 * D : 4 * D]).astype(BF)
        query = dot(normed, att_low[k, 0], ((1,), (0,))) + vec[4 * D : 5 * D]
        query = rotate(query.reshape(-1, HEADS, HD), row_cos, row_sin).astype(BF).reshape(-1, D)
        query = heads_of(query)
        context, log_total = attend_forward(query, keys, values, allowed)
        context = join(context.reshape(n_loss, half))
        branch = dot(context, att_low[k, 1], ((1,), (0,))) + vec[5 * D : 6 * D]
        hidden = dot(feed, ff_low[k, 0], ((1,), (0,))) + vec[7 * D :]
        active = jax.nn.gelu(hidden, approximate=False).astype(BF)
        output = dot(active, ff_low[k, 1], ((1,), (1,))) + vec[6 * D : 7 * D]
        kept.append((normal, scale, normed, feed, query, log_total, context, hidden, active))
        stream = stream + branch + output

    final_normal, final_scale = normal_of(stream)
    picked = (final_normal * final_gain + final_bias).astype(BF)
    logits = dot(picked, unembed, ((1,), (1,)))
    hits = jnp.arange(vr, dtype=jnp.int32)[None, :] == (targets - w * vr)[:, None]
    target_part = jnp.sum(jnp.where(hits, logits, 0.0), axis=1)
    top_part = jnp.max(logits, axis=1)
    total_part = jnp.sum(jnp.exp(logits - top_part[:, None]), axis=1)
    stats = lax.all_gather(jnp.stack([top_part, total_part, target_part]), "wide")
    top = jnp.max(stats[:, 0], axis=0)
    total = jnp.sum(stats[:, 1] * jnp.exp(stats[:, 0] - top), axis=0)
    log_all = top + jnp.log(total)
    loss_sum = jnp.sum(weight * (log_all - jnp.sum(stats[:, 2], axis=0)))
    grad_logits = (jnp.exp(logits - log_all[:, None]) - hits.astype(F4)) * (weight / count)[:, None]
    grad_logits = grad_logits.astype(BF)
    grad_picked = lax.psum(dot(grad_logits, unembed, ((1,), (0,))), "wide")
    grad_unembed = dot(grad_logits, picked, ((0,), (0,)))

    grad_final_gain = jnp.sum(grad_picked * final_normal, axis=0)
    grad_final_bias = jnp.sum(grad_picked, axis=0)
    grad_stream = norm_pull(grad_picked * final_gain, final_normal, final_scale)
    own_rows = D // width

    def own_of(array):
        return lax.dynamic_slice_in_dim(array, w * own_rows, own_rows, axis=1)

    grad_pairs = 0.0
    grad_vectors = [None] * L
    grad_weights = [None] * L
    for k in reversed(range(L)):
        vec = vectors[k]
        normal, scale, normed, feed, query, log_total, context, hidden, active = kept[k]
        grad_low = grad_stream.astype(BF)
        grad_bias_out = jnp.sum(grad_low, axis=0, dtype=F4)
        grad_down = dot(own_of(grad_low), active, ((0,), (0,)))
        grad_active = dot(grad_low, ff_low[k, 1], ((1,), (0,)))
        unused, pull = jax.vjp(partial(jax.nn.gelu, approximate=False), hidden)
        grad_hidden = pull(grad_active)[0].astype(BF)
        grad_bias_up = jnp.sum(grad_hidden, axis=0, dtype=F4)
        grad_up = dot(own_of(feed), grad_hidden, ((0,), (0,)))
        grad_feed = dot(grad_hidden, ff_low[k, 0], ((1,), (1,)))
        grad_out = dot(own_of(context), grad_low, ((0,), (0,)))
        grad_context = dot(grad_low, att_low[k, 1], ((1,), (1,))).astype(BF)
        grad_query, pairs_part = attend_backward(
            query, keys, values, allowed, log_total, heads_of(grad_context)
        )
        grad_pairs = grad_pairs + pairs_part
        grad_query = join(grad_query.reshape(n_loss, half))
        grad_query = rotate(grad_query.astype(F4).reshape(-1, HEADS, HD), row_cos, -row_sin)
        grad_query = grad_query.reshape(-1, D).astype(BF)
        grad_wq = dot(own_of(normed), grad_query, ((0,), (0,)))
        grad_normed = dot(grad_query, att_low[k, 0], ((1,), (1,)))
        grad_vectors[k] = jnp.concatenate(
            [
                jnp.sum(grad_normed * normal, axis=0),
                jnp.sum(grad_normed, axis=0),
                jnp.sum(grad_feed * normal, axis=0),
                jnp.sum(grad_feed, axis=0),
                jnp.sum(grad_query, axis=0, dtype=F4),
                grad_bias_out,
                grad_bias_out,
                grad_bias_up,
            ]
        )
        grad_weights[k] = (grad_wq, grad_out, grad_up, grad_down)
        shaped = grad_normed * vec[:D] + grad_feed * vec[2 * D : 3 * D]
        grad_stream = grad_stream + norm_pull(shaped, normal, scale)

    partial_pairs = grad_pairs.reshape(MICRO, width, width * cap, 2 * HD)
    own_part = lax.dynamic_index_in_dim(partial_pairs, w, 1, False)
    other_part = lax.dynamic_index_in_dim(partial_pairs, w ^ 1, 1, False)
    grad_own = own_part + lax.ppermute(other_part, "wide", swap)
    grad_own = grad_own.reshape(n_slots, 2 * HD).astype(BF).astype(F4)
    turned = rotate(grad_own[:, None, :HD], slot_cos, -slot_sin)[:, 0]
    grad_projected = jnp.concatenate([turned, grad_own[:, HD:]], axis=1).astype(BF)
    own_valid = (own_codes.reshape(-1) < seqs * LEN)
    grad_projected = jnp.where(own_valid[:, None], grad_projected, jnp.zeros((), BF))
    kv_part = dot(slot_normed, grad_projected, ((0,), (0,)))
    slot_grad_normed = dot(grad_projected, kv_low, ((1,), (1,)))
    grad_rows = norm_pull(slot_grad_normed * gain0, slot_normal, slot_scale)
    grad_rows = grad_rows + lax.dot_general(
        pick.astype(F4),
        grad_stream,
        (((0,), (0,)), ((), ())),
        precision=lax.Precision.HIGHEST,
        preferred_element_type=F4,
    )
    grad_rows = jnp.where(own_valid[:, None], grad_rows, 0.0)
    own_ids = jnp.where(
        own_valid, lax.dynamic_index_in_dim(slot_ids, lax.axis_index("rep"), 0, False), vr
    )
    same = own_ids[:, None] == own_ids[None, :]
    order = jnp.arange(n_slots, dtype=jnp.int32)
    earlier = same & (order[None, :] < order[:, None])
    lead = own_valid & ~jnp.any(earlier, axis=1)
    same = same.astype(BF)
    high = grad_rows.astype(BF)
    rest = (grad_rows - high.astype(F4)).astype(BF)
    grad_rows = dot(same, high, ((1,), (0,))) + dot(same, rest, ((1,), (0,)))

    squares = jnp.sum(jnp.where(lead[:, None], grad_rows * grad_rows, 0.0))
    squares = squares + jnp.sum(grad_unembed * grad_unembed)
    for parts in grad_weights:
        for piece in parts:
            squares = squares + jnp.sum(piece * piece)
    kv_total, gain_part, bias_part, pair_bias_grad, square_total = lax.psum(
        (
            kv_part,
            jnp.sum(slot_grad_normed * slot_normal * own_valid[:, None], axis=0),
            jnp.sum(slot_grad_normed * own_valid[:, None], axis=0),
            jnp.sum(grad_projected, axis=0, dtype=F4),
            squares,
        ),
        "wide",
    )
    grad_small = jnp.concatenate(
        [
            grad_vectors[0].at[:D].add(gain_part).at[D : 2 * D].add(bias_part),
            grad_vectors[1],
            pair_bias_grad,
            grad_final_gain,
            grad_final_bias,
        ]
    )
    square_total = square_total + jnp.sum(kv_total * kv_total) + jnp.sum(grad_small * grad_small)
    clip_factor = jnp.minimum(1.0, CLIP / (jnp.sqrt(square_total) + 1e-06))

    un_one, un_two, un_step = moments_step(
        grad_unembed * clip_factor, first_tables[0, 1], second_tables[0, 1]
    )
    un_sum = lax.psum_scatter(
        un_step.astype(BF).reshape(vr, reps, D // reps).transpose(1, 0, 2),
        "rep",
        scatter_dimension=0,
        tiled=True,
    )[0]
    clipped_ids = jnp.minimum(own_ids, vr - 1)
    old_one = jnp.take(first_tables[0, 0], clipped_ids, axis=0)
    old_two = jnp.take(second_tables[0, 0], clipped_ids, axis=0)
    row_one, row_two, row_step = moments_step(grad_rows * clip_factor, old_one, old_two)
    old_step = (BETA_ONE * old_one * FIX_ONE) / (
        jnp.sqrt(BETA_TWO * old_two * FIX_TWO) + ADAM_EPSILON
    )
    em_one = base_one.at[own_ids].set(row_one, mode="drop")
    em_two = base_two.at[own_ids].set(row_two, mode="drop")
    extra = jnp.where(lead[:, None], row_step - old_step.astype(BF).astype(F4), 0.0).astype(BF)
    extra = lax.all_to_all(
        extra.reshape(n_slots, reps, D // reps).transpose(1, 0, 2), "rep", 0, 0, tiled=True
    )
    em_sum = base_sum.astype(F4).at[jnp.where(slot_valid, slot_ids, vr).reshape(-1)].add(
        extra.reshape(reps * n_slots, D // reps).astype(F4), mode="drop"
    )
    table_sum = jnp.stack([em_sum, un_sum.astype(F4)])

    att_grad = jnp.stack([jnp.stack(parts[:2]) for parts in grad_weights])
    ff_grad = jnp.stack([jnp.stack(parts[2:]) for parts in grad_weights])
    kv_grad = lax.dynamic_slice_in_dim(kv_total, w * own_rows, own_rows, axis=0)
    att_one, att_two, att_step = moments_step(
        att_grad * clip_factor, first_attention[0], second_attention[0]
    )
    ff_one, ff_two, ff_step = moments_step(
        ff_grad * clip_factor, first_feedforward[0], second_feedforward[0]
    )
    kv_one, kv_two, kv_step = moments_step(
        kv_grad * clip_factor, first_key_value[0], second_key_value[0]
    )
    sm_one, sm_two, sm_step = moments_step(
        grad_small * clip_factor, first_gains[0], second_gains[0]
    )
    scattered = partial(lax.psum_scatter, axis_name="rep", tiled=True)
    sums = (
        table_sum,
        scattered(att_step.astype(BF), scatter_dimension=3).astype(F4),
        scattered(ff_step.astype(BF), scatter_dimension=3).astype(F4),
        scattered(kv_step, scatter_dimension=1),
        scattered(sm_step, scatter_dimension=0),
    )
    masters = (tables, attention, feedforward, key_value, gains_biases)
    outers = (outer_tables, outer_attention, outer_feedforward, outer_key_value, outer_gains)
    new_masters = []
    new_outers = []
    for index in range(5):
        mean_diff = LEARN_RATES[index] * (sums[index] / reps + DECAY * masters[index])
        momentum = OUTER_MOMENTUM * outers[index] + mean_diff
        new_outers.append(momentum)
        new_masters.append(masters[index] - OUTER_RATE * (mean_diff + OUTER_MOMENTUM * momentum))
    return (
        loss_sum.reshape(1),
        count.reshape(1),
        *new_masters,
        jnp.stack([em_one, un_one])[None],
        att_one[None],
        ff_one[None],
        kv_one[None],
        sm_one[None],
        jnp.stack([em_two, un_two])[None],
        att_two[None],
        ff_two[None],
        kv_two[None],
        sm_two[None],
        *new_outers,
    )


def solution(mesh):
    split = (
        P(None, "wide", "rep"),
        P(None, None, "wide", "rep"),
        P(None, None, "wide", "rep"),
        P("wide", "rep"),
        P("rep"),
    )
    moments = (
        P("rep", None, "wide", None),
        P("rep", None, None, "wide", None),
        P("rep", None, None, "wide", None),
        P("rep", "wide", None),
        P("rep", None),
    )
    tokens = P("rep", None, None, None, None)
    return jax.shard_map(
        body,
        mesh=mesh,
        in_specs=(tokens,) * 3 + split + moments + moments + split,
        out_specs=(P("rep"), P("rep")) + split + moments + moments + split,
        check_vma=False,
    )
```

time: 1930 us -> 891 us (0.46)
  waiting for transfers between devices: 774 us -> 148 us
  matrix products: 340 us -> 144 us
  other arithmetic: 373 us -> 267 us
  blocking collectives: 212 us -> 106 us
  starting transfers between devices: 72.2 us -> 10.4 us
  local copies, waits for them, and re-layouts: 121 us -> 173 us
    reduce_scatter x12 -> x1, waiting for transfers between devices: 362 us -> 0.02 us  [body(): scattered(ff_step.astype(BF), scatter_dimension=3).astype(F4)]
    all_gather x6 -> x5, waiting for transfers between devices: 383 us -> 82.9 us  [the longest x1 58.3 us: body(): ff_low = lax.all_gather(ff_low, 'wide', axis=3, tiled=True)]
    dot_general x84 -> x92, matrix products: 340 us -> 144 us  [the longest x33 84 us: dot(): lax.dot_general(left, right, (dims, ((), ())), preferred_element_type=F4)]
    all_gather x13 -> x5, blocking collectives: 152 us -> 55.7 us  [the longest x1 14.6 us: body(): kv_low = lax.all_gather(kv_low, 'wide', axis=0, tiled=True)]
    all_to_all x16 -> x2, starting transfers between devices: 70.5 us -> 7.77 us  [the longest x1 4.26 us: body(): lax.all_to_all(extra.reshape(n_slots, reps, D // reps).transpose(1, 0, 2)...]
    psum x0 -> x3, waiting for transfers between devices: none -> 55.7 us  [the longest x1 55.7 us: body(): grad_picked = lax.psum(dot(grad_logits, unembed, ((1,), (0,))), 'wide')]
    add x29 -> x16, other arithmetic: 78.3 us -> 23.1 us  [the longest x8 11.3 us: head(): return (so_far + both, (grad_query * 0.125).astype(BF))]
    sub x11 -> x8, other arithmetic: 70.6 us -> 15.6 us  [the longest x5 15 us: body(): masters[index] - OUTER_RATE * (mean_diff + OUTER_MOMENTUM * momentum)]
  transfers between devices with their start and end apart: 35 -> 20, of which waited for: 17 -> 6; matrix products, arithmetic and copies ran while one was open for 34% -> 50% of each run, Pallas kernels for 0% -> 0%
where the time goes in v1:
time: 891 us; the launch traced here: 879 us
  other arithmetic  267 us (30%)
  local copies, waits for them, and re-layouts  173 us (19%)
  waiting for transfers between devices  148 us (17%)
  matrix products  144 us (16%)
  blocking collectives  106 us (12%)
  between operations  28.6 us (3%)
  starting transfers between devices  10.4 us (1%)
    dot_general x33, matrix products, dot(): lax.dot_general(left, right, (dims, ((), ())), preferred_element_type=F4)  84 us
    all_gather x1, waiting for transfers between devices, body(): ff_low = lax.all_gather(ff_low, 'wide', axis=3, tiled=True)  58.3 us
    psum x1, waiting for transfers between devices, body(): grad_picked = lax.psum(dot(grad_logits, unembed, ((1,), (0,))), 'wide')  55.7 us
    another operation x1, other arithmetic, body(): jnp.stack([em_two, un_two])[None]  39.9 us
    unnamed x397, local copies, waits for them, and re-layouts  38.2 us
    unnamed x2, blocking collectives  34.9 us
    while x80, local copies, waits for them, and re-layouts  30 us
    dot_general x16, matrix products, head(): jnp.einsum('mnd,mkd->mnk', query, keys, preferred_element_type=F4) * 0.125  29.4 us
  transfers between devices with their start and end apart: 20, of which 6 were waited for; matrix products, arithmetic and copies ran while one was open for 50% of the time, Pallas kernels for 0%

profile of v1, /device:TPU:0, one launch (start us, length us, event | category | flops | bytes accessed | tf_op | source)
XLA Modules:
  0.0 879.3 jit_solution(12414665085811525909)
XLA Ops:
  10.6 9.7 %all-gather = s32[4,1,2,1,2048]{4,2,3,1,0:T(2,128)S(1)} all-gather(s32[1,1,2,1,2048]{4,2,3,1,0:T(2,128)S(1)} %copy.486), channel_id=2, replica_groups=mesh['rep'=4,'wide'=8] {'rep'}, dimensions={0}, use_global_device_ids=true | all-gather | bytes 81920 | tf_op jit(solution)/shard_map/all_gather | solution.py:179
  23.2 4.5 slice_bitcast_fusion.2
  27.6 12.1 %gather_fusion = bf16[4096,128]{1,0:T(8,128)(2,1)S(1)} fusion(bf16[6288,128]{1,0:T(8,128)(2,1)S(1)} %get-tuple-element.1026, s32[4096]{0:T(1024)S(1)} %broadcast_clamp_fusion), kind=kCustom, calls=%fused_computation.4 | custom fusion | bytes 2113536 | tf_op jit(solution)/shard_map/jit(_take)/gather | solution.py:212
  41.7 3.5 all-to-all-start
  49.5 7.8 all-to-all-done
  58.6 9.9 %all-gather.1 = bf16[8,2,64,128]{3,2,1,0:T(8,128)(2,1)} all-gather(bf16[2,2,64,128]{3,2,1,0:T(8,128)(2,1)S(1)} %convert_element_type.289), channel_id=3, replica_groups=mesh['rep'=4,'wide'=8] {'rep'}, dimensions={0}, use_global_device_ids=true | all-gather | bytes 327680 | tf_op jit(solution)/shard_map/all_gather | solution.py:167
  70.4 16.0 %all-reduce.2 = f32[12416]{0:T(1024)S(1)} all-reduce(f32[12416]{0:T(1024)S(1)} %dynamic-update-slice.4), channel_id=1, replica_groups=mesh['rep'=4,'wide'=8] {'rep'}, use_global_device_ids=true, to_apply=%add.2 | all-reduce | flops 12416 | bytes 99328
  86.5 7.3 all_gather.47
  94.0 14.6 %all_gather.48 = bf16[512,128]{1,0:T(8,128)(2,1)S(1)} all-gather(bf16[64,128]{1,0:T(8,128)(2,1)S(1)} %copy.363), channel_id=1, replica_groups=mesh['rep'=4,'wide'=8] {'wide'}, dimensions={0}, use_global_device_ids=true | all-gather | bytes 147456 | tf_op jit(solution)/shard_map/all_gather | solution.py:172
  132.9 9.2 %all-gather.14.cloned.1.call-done = bf16[2,8,512,128]{3,2,0,1:T(8,128)(2,1)} async-done(((bf16[2,1,512,128]{3,2,0,1:T(8,128)(2,1)}), bf16[2,8,512,128]{3,2,0,1:T(8,128)(2,1)}) %all-gather.14.cloned.1.call-update) | async-done | bytes 2097168 | tf_op jit(solution)/shard_map/all_gather | solution.py:224
  148.7 13.1 %while.54 = (s32[]{:T(128)}, bf16[4,2,128,64]{2,3,1,0:T(8,128)(2,1)S(1)}, f32[4,2,128,1]{2,1,3,0:T(2,128)S(1)}, bf16[4,2,128,64]{2,3,1,0:T(8,128)(2,1)S(1)}, bf1...) while((s32[]{:T(128)}, ...), condition=%wide.region_10.12_spmd.clone, body=%wide.region_7.11_spmd.clone.sunk | while | flops 279985920 | bytes 14788729 | solution.py:91
  166.8 58.3 %all-gather.16.cloned.1.call-done = bf16[4,2,2,512,512]{4,3,2,1,0:T(8,128)(2,1)} async-done(((bf16[4,2,2,64,512]{4,3,2,1,0:T(8,128)(2,1)}), bf16[4,2,2,512,512]{4,3,2,1,0:T(8,128)(2,1)}) %all-gather.16.cloned.1.call-update) | async-done | bytes 8388624 | tf_op jit(solution)/shard_map/all_gather | solution.py:171
  225.1 13.5 %copy.373 = bf16[2,2,512,4,512]{2,4,3,1,0:T(8,128)(2,1)} copy(bf16[2,2,512,4,512]{4,2,1,0,3:T(8,128)(2,1)} %bitcast.661) | data formatting | bytes 16777216 | tf_op jit(solution)/shard_map/transpose | solution.py:174
  238.7 7.7 multiply_convert_fusion.4
  255.6 13.3 %while.55 = (s32[]{:T(128)}, bf16[4,2,128,64]{2,3,1,0:T(8,128)(2,1)S(1)}, f32[4,2,128,1]{2,1,3,0:T(2,128)S(1)}, bf16[4,2,128,64]{2,3,1,0:T(8,128)(2,1)S(1)}, bf1...) while((s32[]{:T(128)}, ...), condition=%wide.region_16.18_spmd.clone, body=%wide.region_13.17_spmd.clone.sunk | while | flops 279985920 | bytes 14788729 | solution.py:91
  269.4 7.7 multiply_convert_fusion.3
  281.7 15.4 %all-gather.20.cloned.1.call-done = bf16[1,6288,512]{2,1,0:T(8,128)(2,1)} async-done(((bf16[1,6288,128]{2,1,0:T(8,128)(2,1)}), bf16[1,6288,512]{2,1,0:T(8,128)(2,1)}) %all-gather.20.cloned.1.call-update) | async-done | bytes 6438928 | tf_op jit(solution)/shard_map/all_gather | solution.py:175
  297.2 4.8 fusion.287
  303.7 14.2 %all-gather.5 = f32[8,3,256]{2,1,0:T(4,128)S(1)} all-gather(f32[1,3,256]{2,1,0:T(4,128)S(1)} %maximum_bitcast_fusion.3), channel_id=6, replica_groups=mesh['rep'=4,'wide'=8] {'wide'}, dimensions={0}, use_global_device_ids=true | all-gather | bytes 27648 | tf_op jit(solution)/shard_map/all_gather | solution.py:301
  322.4 55.7 %all-reduce.13.cloned.1.call-done = f32[256,512]{1,0:T(8,128)} async-done(((f32[256,512]{1,0:T(8,128)}), f32[256,512]{1,0:T(8,128)}) %all-reduce.13.cloned.1.call-update) | async-done | bytes 524304 | tf_op jit(solution)/shard_map/psum | solution.py:308
  384.3 46.3 %while.56 = (s32[]{:T(128)}, f32[2,4096,128]{1,2,0:T(8,128)}, bf16[4,2,128,64]{2,3,1,0:T(8,128)(2,1)S(1)}, bf16[4,2,128,64]{2,3,1,0:T(8,128)(2,1)S(1)}, bf16[2,4...) while((s32[]{:T(128)}, f32[2,4096,128]{1,2,0:T(8,128)}, ...), condition=%wide.region_34.37_spmd.clone, body=%wide.region_32.36_spmd.clone.sunk | while | flops 687374080 | bytes 85343536 | solution.py:113
  430.9 4.8 convert_reduce_fusion.1
  437.1 3.2 multiply_reduce_fusion.8
  442.8 46.7 %while.57 = (s32[]{:T(128)}, f32[2,4096,128]{1,2,0:T(8,128)}, bf16[4,2,128,64]{2,3,1,0:T(8,128)(2,1)S(1)}, bf16[4,2,128,64]{2,3,1,0:T(8,128)(2,1)S(1)}, bf16[2,4...) while((s32[]{:T(128)}, f32[2,4096,128]{1,2,0:T(8,128)}, ...), condition=%wide.region_39.42_spmd.clone, body=%wide.region_37.41_spmd.clone.sunk | while | flops 687374080 | bytes 85343536 | solution.py:113
  489.5 4.0 add.771
  493.5 3.8 copy.423
  503.5 25.0 %slice_bitcast_fusion.1 = (f32[6288,512]{1,0:T(8,128)}, bf16[1,1,6288,512]{3,2,1,0:T(8,128)(2,1)}, f32[6288,512]{1,0:T(8,128)}) fusion(f32[1,2,6288,512]{3,2,1,0:T(8,128)} %param.47, f32[1,2,6288,512]{3,2,1,0:T(8,128)} %param.52), kind=kLoop, calls=%fused_computation.95 | loop fusion | flops 16097280 | bytes 57950208 | tf_op jit(solution)/shard_map/squeeze | solution.py:157
  528.5 11.9 %div.204 = bf16[6288,4,128]{2,1,0:T(4,128)(2,1)} reshape(bf16[1,1,6288,512]{3,2,1,0:T(8,128)(2,1)} %get-tuple-element.1024) | data formatting | bytes 12877824 | tf_op jit(solution)/shard_map/div | solution.py:159
  540.5 6.3 copy.479
  548.6 12.4 %multiply_reduce_fusion.2 = (f32[]{:T(128)}, f32[6288,512]{1,0:T(8,128)}) fusion(f32[256,512]{1,0:T(8,128)S(1)} %copy-done.6, f32[512]{0:T(512)S(1)} %copy-done.70, f32[512]{0:T(512)S(1)} %copy-done.64, f32[256]{0:T(256)S(1)} %copy-done.62, f32[256]{0:T(256)S(1)} %copy-done.60, f32[256,6288]{0,1:T(8,128)} %copy-done.4, f32[256]{0:T(256)S(1)} %copy-done.117, ...), kind=kOutput, calls=%fused_computation.92 | convolution fusion | flops 1665114112 | bytes 19850244 | tf_op jit(solution)/shard_map/dot_general | solution.py:35
  570.6 3.5 convert_reduce_fusion.2
  603.8 15.7 %all-reduce.6 = (f32[]{:T(128)}, f32[512]{0:T(512)S(1)}, f32[512]{0:T(512)S(1)}, f32[128]{0:T(128)S(1)}) all-reduce(f32[]{:T(128)S(6)} %add.789, f32[512]{0:T(512)} %get-tuple-element.854, f32[512]{0:T(512)} %get-tuple-element.856, f32[128]{0:T(128)} %convert_reduce_fusion.3), channel_id=1, replica_groups=mesh['rep'=4,'wide'=8] {'wide'}, use_global_device_ids=true, to_apply=%region_54.57 | all-reduce | flops 1153 | bytes 9224 | tf_op jit(solution)/shard_map/psum | solution.py:398
  650.9 5.3 fusion.100
  656.3 39.9 %fusion.101 = (f32[1,6288,512]{2,1,0:T(8,128)}, bf16[786,4,8,128]{3,2,1,0:T(8,128)(2,1)}, f32[1,6288,512]{2,1,0:T(8,128)}, f32[6288,512]{1,0:T(8,128)}, f32[6288,512]{1,0:T(8,128)}) fusion(f32[6288,512]{1,0:T(8,128)} %get-tuple-element.1127, f32[]{:T(128)S(6)} %min_shard_map.3, f32[1,2,6288,512]{3,2,1,0:T(8,128)} %param.52, f32[1,2,6288,512]{3,2,1,0:T(8,128)} %param.47), kind=kLoop, calls=%fused_computation.210 | loop fusion | flops 48291840 | bytes 122339328 | tf_op jit(solution)/shard_map/stack | solution.py:488
  696.2 6.7 copy.478
  703.6 10.1 %gather_fusion.3 = f32[1024,512]{1,0:T(8,128)} fusion(f32[6288,512]{1,0:T(8,128)} %get-tuple-element.1023, s32[1024]{0:T(1024)S(1)} %fusion.244), kind=kCustom, calls=%fused_computation.1.clone | custom fusion | bytes 4198400 | tf_op jit(solution)/shard_map/jit(_take)/gather | solution.py:430
  713.7 10.0 %gather_fusion.4 = f32[1024,512]{1,0:T(8,128)} fusion(f32[6288,512]{1,0:T(8,128)} %get-tuple-element.1025, s32[1024]{0:T(1024)S(1)} %fusion.244), kind=kCustom, calls=%fused_computation.3.clone | custom fusion | bytes 4198400 | tf_op jit(solution)/shard_map/jit(_take)/gather | solution.py:431
  724.4 3.3 bitcast_convert_fusion
  728.0 5.8 bitcast_bitcast_fusion.1
  733.8 4.3 all-to-all-start.1
  738.1 15.4 %scatter_custom_fusion.1 = f32[6288,512]{1,0:T(8,128)} fusion(f32[6288,512]{1,0:T(8,128)} %get-tuple-element.1021, s32[1024]{0:T(1024)} %bitcast.743, f32[1024,512]{1,0:T(8,128)} %gather_fusion.3, f32[1024,512]{1,0:T(8,128)S(1)} %get-tuple-element.1125, f32[]{:T(128)} %constant.235.clone.1, f32[]{:T(128)} %constant.449.clone.1, f32[]{:T(128)S(6)} %min_shard_map.3, ...), kind=kCustom, calls=%fused_computation.240 | custom fusion | flops 2621440 | bytes 17074692 | tf_op jit(solution)/shard_map/scatter | solution.py:436
  753.5 15.7 %scatter_custom_fusion.2 = f32[6288,512]{1,0:T(8,128)} fusion(f32[6288,512]{1,0:T(8,128)} %get-tuple-element.1022, s32[1024]{0:T(1024)} %bitcast.744, f32[1024,512]{1,0:T(8,128)} %gather_fusion.4, f32[1024,512]{1,0:T(8,128)S(1)} %get-tuple-element.1125, f32[]{:T(128)} %constant.235.clone.1, f32[]{:T(128)} %constant.454.clone.1, f32[]{:T(128)} %constant.453.clone.1, ...), kind=kCustom, calls=%fused_computation.241 | custom fusion | flops 3145728 | bytes 17074692 | tf_op jit(solution)/shard_map/scatter | solution.py:437
  770.1 18.9 %all-reduce.5 = f32[12416]{0:T(1024)S(1)} all-reduce(f32[12416]{0:T(1024)S(1)} %fusion.190), channel_id=12, replica_groups=mesh['rep'=4,'wide'=8] {'rep'}, use_global_device_ids=true, to_apply=%region_85.88.clone | all-reduce | flops 12416 | bytes 99328
  789.0 5.6 fusion.82
  794.7 20.6 %maximum_bitcast_fusion.1 = f32[1,2,6288,512]{3,2,1,0:T(8,128)} fusion(f32[1,6288,512]{2,1,0:T(8,128)} %get-tuple-element.1018, f32[1,6288,512]{2,1,0:T(8,128)} %bitcast.636), kind=kLoop, calls=%fused_computation.87 | loop fusion | flops 6438912 | bytes 51511296 | tf_op jit(solution)/shard_map/broadcast_in_dim | solution.py:488
  819.5 9.2 %maximum_bitcast_fusion = f32[1,2,6288,512]{3,2,1,0:T(8,128)} fusion(f32[1,6288,512]{2,1,0:T(8,128)S(1)} %bitcast.635, f32[1,6288,512]{2,1,0:T(8,128)S(1)} %bitcast.639), kind=kLoop, calls=%fused_computation.86 | loop fusion | flops 6438912 | bytes 51511296 | tf_op jit(solution)/shard_map/broadcast_in_dim | solution.py:483
  834.7 23.9 %scatter_custom_fusion = f32[6288,128]{1,0:T(8,128)S(1)} fusion(f32[6288,128]{1,0:T(8,128)S(1)} %copy-done.11, s32[4096]{0:T(1024)} %bitcast.730, bf16[4096,128]{1,0:T(8,128)(2,1)} %bitcast.149), kind=kCustom, calls=%fused_computation.156 | custom fusion | flops 1048576 | bytes 4268032 | tf_op jit(solution)/shard_map/scatter-add | solution.py:442
  862.7 8.8 %multiply_subtract_fusion = (f32[2,6288,128]{2,1,0:T(8,128)}, f32[2,6288,128]{2,1,0:T(8,128)}) fusion(f32[2,6288,128]{2,1,0:T(8,128)} %param.42, f32[1,6288,128]{2,1,0:T(8,128)S(1)} %convert_element_type.341, f32[1,6288,128]{2,1,0:T(8,128)S(1)} %bitcast.652, f32[2,6288,128]{2,1,0:T(8,128)} %param.57), kind=kLoop, calls=%fused_computation.110 | loop fusion | flops 17707008 | bytes 32194560 | tf_op jit(solution)/shard_map/sub | solution.py:478
  (851 shorter events, 283.1 us)
Async XLA Ops:
  8.0 104.9 %all-gather.18.cloned.1.call-start = ((), (), s32[]{:S(2)}) async-start(), calls=%async_computation.14 | async-start | bytes 1310720 | tf_op jit(solution)/shard_map/all_gather | solution.py:168
  41.7 15.5 %all-to-all-start = ((bf16[4,1024,128]{2,1,0:T(8,128)(2,1)}), bf16[4,1024,128]{2,1,0:T(8,128)(2,1)S(1)}, u32[]{:S(2)}, u32[]{:S(2)}) async-start(bf16[4,1024,128]{2,1,0:T(8,128)(2,1)} %select_convert_fusion.1), calls=%async_computation | async-start | bytes 2097152 | tf_op jit(solution)/shard_map/all_to_all | solution.py:214
  45.3 79.5 %all-reduce.11.cloned.1.call-start = ((), (), s32[]{:S(2)}) async-start(), calls=%async_computation.7 | async-start | bytes 1048576 | tf_op jit(solution)/shard_map/psum | solution.py:255
  48.4 20.2 %copy-start.167 = (u32[32]{0:T(128)S(1)}, u32[32]{0:T(128)}, u32[]{:S(2)}) copy-start(u32[32]{0:T(128)} %constant.505) | copy-start | bytes 388
  49.1 20.8 %copy-start.71 = (f32[3104]{0:T(1024)S(1)}, f32[3104]{0:T(1024)}, u32[]{:S(2)}) copy-start(f32[3104]{0:T(1024)} %param.46) | copy-start | bytes 37252
  49.4 37.0 %copy-start.75 = (pred[128,512]{1,0:T(32,128)(4,1)}, pred[128,512]{1,0:T(32,128)(4,1)S(1)}, u32[]{:S(2)}) copy-start(pred[128,512]{1,0:T(32,128)(4,1)S(1)} %get-tuple-element.1148) | copy-start | bytes 196612
  49.4 37.0 %copy-start.77 = (pred[128,512]{1,0:T(32,128)(4,1)}, pred[128,512]{1,0:T(32,128)(4,1)S(1)}, u32[]{:S(2)}) copy-start(pred[128,512]{1,0:T(32,128)(4,1)S(1)} %get-tuple-element.1149) | copy-start | bytes 196612
  57.3 52.1 %copy-start.7 = (bf16[4,1024,128]{2,1,0:T(8,128)(2,1)}, bf16[4,1024,128]{2,1,0:T(8,128)(2,1)S(1)}, u32[]{:S(2)}) copy-start(bf16[4,1024,128]{2,1,0:T(8,128)(2,1)S(1)} %all-to-all-done) | copy-start | bytes 3145732
  57.3 29.2 %copy-start.73 = (f32[64,32]{0,1:T(8,128)S(1)}, f32[64,32]{0,1:T(8,128)}, u32[]{:S(2)}) copy-start(f32[64,32]{0,1:T(8,128)} %param.45) | copy-start | bytes 24580
  58.5 70.0 %all-gather.12.cloned.1.call-start = ((), (), s32[]{:S(2)}) async-start(), calls=%async_computation.8 | async-start | bytes 2359296 | tf_op jit(solution)/shard_map/all_gather | solution.py:170
  68.6 73.5 %all-gather.14.cloned.1.call-start = ((), (), s32[]{:S(2)}) async-start(), calls=%async_computation.9 | async-start | bytes 2359296 | tf_op jit(solution)/shard_map/all_gather | solution.py:224
  86.5 23.3 %copy-start.88 = (s32[1024]{0:T(1024)}, s32[1024]{0:T(1024)S(1)}, u32[]{:S(2)}) copy-start(s32[1024]{0:T(1024)S(1)} %reshape.1332) | copy-start | bytes 12292
  112.9 112.2 %all-gather.16.cloned.1.call-start = ((), (), s32[]{:S(2)}) async-start(), calls=%async_computation.10 | async-start | bytes 9437184 | tf_op jit(solution)/shard_map/all_gather | solution.py:171
  113.5 183.7 %all-gather.20.cloned.1.call-start = ((), (), s32[]{:S(2)}) async-start(), calls=%async_computation.15 | async-start | bytes 8048640 | tf_op jit(solution)/shard_map/all_gather | solution.py:175
  114.1 264.0 %all-reduce.13.cloned.1.call-start = ((), (), s32[]{:S(2)}) async-start(), calls=%async_computation.11 | async-start | bytes 1048576 | tf_op jit(solution)/shard_map/psum | solution.py:308
  128.5 110.1 %copy-start.55 = (bf16[256,512]{1,0:T(8,128)(2,1)}, bf16[256,512]{1,0:T(8,128)(2,1)S(1)}, u32[]{:S(2)}) copy-start(bf16[256,512]{1,0:T(8,128)(2,1)S(1)} %get-tuple-element.1044) | copy-start | bytes 786436
  161.9 76.8 %copy-start.42 = (bf16[4,2,128,64]{2,3,1,0:T(8,128)(2,1)}, bf16[4,2,128,64]{2,3,1,0:T(8,128)(2,1)S(1)}, u32[]{:S(2)}) copy-start(bf16[4,2,128,64]{2,3,1,0:T(8,128)(2,1)S(1)} %get-tuple-element.1597) | copy-start | bytes 393220
  162.5 1.4 collective-permute-start
  269.1 8.0 collective-permute-start.1
  279.1 18.1 %copy-start.63 = (f32[512]{0:T(512)S(1)}, f32[512]{0:T(512)}, u32[]{:S(2)}) copy-start(f32[512]{0:T(512)} %get-tuple-element.1070) | copy-start | bytes 6148
  281.5 98.6 %copy-start.5 = (f32[256,512]{1,0:T(8,128)}, f32[256,512]{1,0:T(8,128)S(1)}, u32[]{:S(2)}) copy-start(f32[256,512]{1,0:T(8,128)S(1)} %get-tuple-element.1120) | copy-start | bytes 1572868
  281.5 98.5 %copy-start.59 = (f32[256]{0:T(256)}, f32[256]{0:T(256)S(1)}, u32[]{:S(2)}) copy-start(f32[256]{0:T(256)S(1)} %broadcast_multiply_fusion.11) | copy-start | bytes 3076
  281.7 98.3 %copy-start.61 = (f32[256]{0:T(256)}, f32[256]{0:T(256)S(1)}, u32[]{:S(2)}) copy-start(f32[256]{0:T(256)S(1)} %add_rsqrt_fusion.1) | copy-start | bytes 3076
  322.1 316.4 %all-reduce.15.cloned.1.call-start = ((), (), s32[]{:S(2)}) async-start(), calls=%async_computation.12 | async-start | bytes 524288 | tf_op jit(solution)/shard_map/psum | solution.py:398
  382.7 48.2 %copy-start.20 = (bf16[256,512]{1,0:T(8,128)(2,1)}, bf16[256,512]{1,0:T(8,128)(2,1)S(1)}, u32[]{:S(2)}) copy-start(bf16[256,512]{1,0:T(8,128)(2,1)S(1)} %get-tuple-element.978) | copy-start | bytes 786436
  430.8 5.0 collective-permute-start.2
  498.8 2.6 collective-permute-start.3
  501.4 45.9 %copy-start.108 = (s32[1024]{0:T(1024)}, s32[1024]{0:T(1024)S(1)}, u32[]{:S(2)}) copy-start(s32[1024]{0:T(1024)S(1)} %get-tuple-element.975) | copy-start | bytes 12292
  501.4 46.5 %copy-start.120 = (pred[1024]{0:T(1024)(128)(4,1)}, pred[1024]{0:T(1024)(128)(4,1)S(1)}, u32[]{:S(2)}) copy-start(pred[1024]{0:T(1024)(128)(4,1)S(1)} %get-tuple-element.976) | copy-start | bytes 3076
  502.0 26.5 %copy-start.51 = (bf16[1024,64]{0,1:T(8,128)(2,1)}, bf16[1024,64]{0,1:T(8,128)(2,1)S(1)}, u32[]{:S(2)}) copy-start(bf16[1024,64]{0,1:T(8,128)(2,1)S(1)} %get-tuple-element.1062) | copy-start | bytes 393220
  503.5 220.9 %reduce-scatter.20.cloned.1.call-start = ((), (), s32[]{:S(2)}) async-start(), calls=%async_computation.18 | async-start | bytes 8048640
  546.9 283.8 %reduce-scatter.18.cloned.1.call-start = ((), (), s32[]{:S(2)}) async-start(), calls=%async_computation.17 | async-start | bytes 81920
  567.5 12.3 %collective-permute-start.4 = (bf16[256,256]{0,1:T(8,128)(2,1)}, bf16[256,256]{0,1:T(8,128)(2,1)}, u32[]{:S(2)}, u32[]{:S(2)}) collective-permute-start(bf16[256,256]{0,1:T(8,128)(2,1)} %bitcast.561), channel_id=1, source_target_pairs={{0,1},{1,0},{2,3},{3,2},{4,5},{5,4},{6,7},{7,6},{8,9},{9,8},{10,11... | collective-permute-start | bytes 393224 | tf_op jit(solution)/shard_map/ppermute | solution.py:268
  593.8 36.2 %copy-start.79 = (f32[512]{0:T(512)S(1)}, f32[512]{0:T(512)}, u32[]{:S(2)}) copy-start(f32[512]{0:T(512)} %get-tuple-element.977) | copy-start | bytes 6148
  593.8 38.8 %copy-start.96 = (f32[2048]{0:T(1024)S(1)}, f32[2048]{0:T(1024)}, u32[]{:S(2)}) copy-start(f32[2048]{0:T(1024)} %get-tuple-element.1146) | copy-start | bytes 24580
  593.8 41.9 %copy-start.99 = (f32[512]{0:T(512)S(1)}, f32[512]{0:T(512)}, u32[]{:S(2)}) copy-start(f32[512]{0:T(512)} %get-tuple-element.871) | copy-start | bytes 6148
  644.3 187.6 %reduce-scatter.16.cloned.1.call-start = ((), (), s32[]{:S(2)}) async-start(), calls=%async_computation.16 | async-start | bytes 327680
  650.9 207.7 %reduce-scatter.14.cloned.1.call-start = ((), (), s32[]{:S(2)}) async-start(), calls=%async_computation.13 | async-start | bytes 1310720 | tf_op jit(solution)/shard_map/reduce_scatter | solution.py:466
  656.3 204.8 %reduce-scatter.22.cloned.1.call-start = ((), (), s32[]{:S(2)}) async-start(), calls=%async_computation.19 | async-start | bytes 8048640
  733.8 100.9 %all-to-all-start.1 = ((bf16[4,1024,128]{2,1,0:T(8,128)(2,1)}), bf16[4,1024,128]{2,1,0:T(8,128)(2,1)}, u32[]{:S(2)}, u32[]{:S(2)}) async-start(bf16[4,1024,128]{2,1,0:T(8,128)(2,1)} %bitcast_bitcast_fusion.1), calls=%async_computation.1 | async-start | bytes 2097152 | tf_op jit(solution)/shard_map/all_to_all | solution.py:439
  794.6 20.6 %slice-start = ((s8[12877824]{0:T(1024)(128)(4,1)}), s8[4194304]{0:T(1024)(128)(4,1)S(1)}, s32[]{:S(2)}) async-start(s8[12877824]{0:T(1024)(128)(4,1)} %bitcast.634), calls=%async_computation.20 | async-start | bytes 8388608
  794.6 20.6 %slice-start.4 = ((s8[12877824]{0:T(1024)(128)(4,1)}), s8[4194304]{0:T(1024)(128)(4,1)S(1)}, s32[]{:S(2)}) async-start(s8[12877824]{0:T(1024)(128)(4,1)} %bitcast.637), calls=%async_computation.24 | async-start | bytes 8388608
  794.6 20.6 %slice-start.1 = ((s8[12877824]{0:T(1024)(128)(4,1)}), s8[4194304]{0:T(1024)(128)(4,1)S(1)}, s32[]{:S(2)}) async-start(s8[12877824]{0:T(1024)(128)(4,1)} %bitcast.634), calls=%async_computation.21 | async-start | bytes 8388608
  794.6 22.3 %slice-start.2 = ((s8[12877824]{0:T(1024)(128)(4,1)}), s8[4194304]{0:T(1024)(128)(4,1)S(1)}, s32[]{:S(2)}) async-start(s8[12877824]{0:T(1024)(128)(4,1)} %bitcast.634), calls=%async_computation.22 | async-start | bytes 8388608
  794.7 22.3 %slice-start.3 = ((s8[12877824]{0:T(1024)(128)(4,1)}), s8[294912]{0:T(1024)(128)(4,1)S(1)}, s32[]{:S(2)}) async-start(s8[12877824]{0:T(1024)(128)(4,1)} %bitcast.634), calls=%async_computation.23 | async-start | bytes 589824
  794.7 23.6 %slice-start.5 = ((s8[12877824]{0:T(1024)(128)(4,1)}), s8[4194304]{0:T(1024)(128)(4,1)S(1)}, s32[]{:S(2)}) async-start(s8[12877824]{0:T(1024)(128)(4,1)} %bitcast.637), calls=%async_computation.25 | async-start | bytes 8388608
  794.7 24.8 %slice-start.6 = ((s8[12877824]{0:T(1024)(128)(4,1)}), s8[4194304]{0:T(1024)(128)(4,1)S(1)}, s32[]{:S(2)}) async-start(s8[12877824]{0:T(1024)(128)(4,1)} %bitcast.637), calls=%async_computation.26 | async-start | bytes 8388608
  794.7 24.7 %slice-start.7 = ((s8[12877824]{0:T(1024)(128)(4,1)}), s8[294912]{0:T(1024)(128)(4,1)S(1)}, s32[]{:S(2)}) async-start(s8[12877824]{0:T(1024)(128)(4,1)} %bitcast.637), calls=%async_computation.27 | async-start | bytes 589824
  (185 other events, 855.1 us)
Sparse Core Ops, SparseCore 0:
  11.3 29.3 all-gather.17
  68.7 30.6 all-gather.11
  113.0 28.9 all-gather.13
  143.5 81.5 all-gather.15
  227.3 69.7 all-gather.19
  547.0 71.1 reduce-scatter.19
  644.5 21.8 reduce-scatter.17
  669.3 24.1 reduce-scatter.15
  696.4 27.6 reduce-scatter.13
  727.9 85.2 reduce-scatter.21
Sparse Core Ops, SparseCore 1:
  58.6 66.1 all-reduce.10
  322.2 55.9 all-reduce.12
  503.6 53.8 all-reduce.14
